TPU v7x, 256 devices: a whole 4x4x8 slice. The times are simulated.
256 devices in a mesh: lev: 8 (over y, z_hi), gy: 4 (over x), gx: 8 (over z_lo, core).
Axes of the slice: x: 4, y: 4, z: 8 (z_hi: 2, z_lo: 4; z = z_hi * 4 + z_lo), core: 2. Of those that a mesh axis runs over, the one named last changes fastest.
Arguments:
- fields: bfloat16 [320, 256, 2048], P('lev', 'gy', 'gx'), may hold values from -6 to 6
- sea_mask: int32 [256, 2048], P('gy', 'gx'), may hold values 0 or 1
- fold_partner: int32 [2048], replicated, may hold values from 0 to 2047, as said below
- embed_weight: bfloat16 [320, 192], P('lev'), may hold values from -0.3125 to 0.3125
- dw_weight: float32 [2, 192, 7, 7], P(None, 'lev'), may hold values from -0.875 to 0.875
- ln_gain: bfloat16 [2, 192], P(None, 'lev'), may hold values from 0.099609375 to 1.8984375
- up_weight: bfloat16 [2, 768, 192], P(None, 'lev'), may hold values from -0.4375 to 0.4375
- down_weight: bfloat16 [2, 768, 192], P(None, 'lev'), may hold values from -0.21875 to 0.21875
Outputs:
- encoded: bfloat16 [192, 256, 2048], P('lev', 'gy', 'gx')
Inputs may be any that keep to these rules, and one draw needn't show every extreme that they name: fold_partner[fold_partner[i]] = i: the columns pair up across the north fold.
All inputs are finite; a program needn't handle non-finite values. No bound on the sum of `sea_mask` on one device may be relied on, other than what follows from the above.
Results may differ from a plain program's by a relative error of at most 0.027.
Values may be sent and summed in bfloat16 or wider, within the bound.
A program may use at most 64 MiB of HBM per device.

v0:
```python
import jax
import jax.numpy as jnp
from jax import lax
from jax.sharding import PartitionSpec as P

BLOCKS = 2


def extended_2(cells, sides, width, closed):
    for axis, dim in sides:
        count = lax.axis_size(axis)
        ends = count if closed else count - 1
        head = lax.slice_in_dim(cells, 0, width, axis=dim)
        tail = lax.slice_in_dim(cells, cells.shape[dim] - width, cells.shape[dim], axis=dim)
        cells = jnp.concatenate(
            [
                lax.ppermute(tail, axis, [(i, (i + 1) % count) for i in range(ends)]),
                cells,
                lax.ppermute(head, axis, [((i + 1) % count, i) for i in range(ends)]),
            ],
            axis=dim,
        )
    return cells


def rounded(values):
    return lax.optimization_barrier(values.astype(jnp.bfloat16)).astype(jnp.float32)


def depthwise(padded, kernel, height, width):
    total = jnp.zeros((padded.shape[0], height, width), jnp.float32)
    for row_off in range(7):
        for col_off in range(7):
            tap = kernel[:, row_off, col_off][:, None, None]
            total = total + tap * padded[
                :, row_off : row_off + height, col_off : col_off + width
            ].astype(jnp.float32)
    return total


def body(fields, sea_mask, fold_partner, embed_weight, dw_weight, ln_gain, up_weight, down_weight):
    in_local, height, width = fields.shape
    lev_count = lax.axis_size("lev")
    chan_local = dw_weight.shape[1]
    channels = chan_local * lev_count
    cells = height * width
    sea = sea_mask.astype(jnp.float32)
    total_cols = width * lax.axis_size("gx")
    at_north = lax.axis_index("gy") == lax.axis_size("gy") - 1
    flat = fields.reshape(in_local, cells)
    stem_part = lax.dot_general(
        embed_weight, flat, (((0,), (0,)), ((), ())), preferred_element_type=jnp.float32
    )
    stem = lax.psum_scatter(
        rounded(stem_part).astype(jnp.bfloat16), "lev", scatter_dimension=0, tiled=True
    ).astype(jnp.float32)
    state = (sea * stem.reshape(chan_local, height, width)).astype(jnp.bfloat16)
    col_ids = jnp.mod(
        lax.axis_index("gx") * width - 3 + jnp.arange(width + 6, dtype=jnp.int32), total_cols
    )
    fold_cols = fold_partner[col_ids]
    for block in range(BLOCKS):
        ext_rows = extended_2(state, (("gy", 1),), 3, False)
        extended = extended_2(ext_rows, (("gx", 2),), 3, True)
        rim = state[:, height - 3 :, :]
        whole_rim = lax.all_gather(rim, "gx", axis=2, tiled=True)
        fold_rows = jnp.take(whole_rim[:, ::-1, :], fold_cols, axis=2)
        folded = jnp.concatenate([extended[:, : height + 3, :], fold_rows], axis=1)
        extended = jnp.where(at_north, folded, extended)
        conv = depthwise(extended, dw_weight[block], height, width)
        sum_one, sum_two = (
            lax.psum(jnp.sum(conv, axis=0).astype(jnp.bfloat16), "lev").astype(jnp.float32),
            lax.psum(jnp.sum(conv * conv, axis=0).astype(jnp.bfloat16), "lev").astype(jnp.float32),
        )
        mean_val = sum_one / channels
        var_val = sum_two / channels - mean_val * mean_val
        gain = ln_gain[block].astype(jnp.float32)[:, None, None]
        normed = ((conv - mean_val) * lax.rsqrt(var_val + 1e-06) * gain).astype(jnp.bfloat16)
        up_local = up_weight[block]
        down_local = down_weight[block]
        pre = jnp.dot(
            up_local,
            lax.all_gather(normed.reshape(chan_local, cells), "lev", axis=0, tiled=True),
            preferred_element_type=jnp.float32,
        )
        hidden = jax.nn.gelu(pre, approximate=True).astype(jnp.bfloat16)
        part = lax.dot_general(
            down_local, hidden, (((0,), (0,)), ((), ())), preferred_element_type=jnp.float32
        )
        branch = (
            lax.psum_scatter(
                rounded(part).astype(jnp.bfloat16), "lev", scatter_dimension=0, tiled=True
            )
            .astype(jnp.float32)
            .reshape(chan_local, height, width)
        )
        state = (sea * (state.astype(jnp.float32) + branch)).astype(jnp.bfloat16)
    return state


def solution(mesh):
    in_specs = (
        P("lev", "gy", "gx"),
        P("gy", "gx"),
        P(),
        P("lev", None),
        P(None, "lev", None, None),
        P(None, "lev"),
        P(None, "lev", None),
        P(None, "lev", None),
    )
    out_specs = P("lev", "gy", "gx")
    return jax.shard_map(body, mesh=mesh, in_specs=in_specs, out_specs=out_specs, check_vma=False)
```

profile of v0, /device:TPU:127, one launch (start us, length us, event | category | flops | bytes accessed | tf_op | source)
XLA Modules:
  0.0 1100.7 jit_solution(17015705490269540974)
XLA Ops:
  6.5 2.1 copy.44
  8.6 4.5 convolution_convert_fusion.2
  13.2 0.7 copy-done.10
  14.0 2.2 gather_fusion
  16.3 0.6 copy_bitcast_fusion
  16.9 0.6 slice_bitcast_fusion.95
  17.5 0.7 slice_bitcast_fusion.96
  18.2 0.7 slice_bitcast_fusion.97
  18.9 144.2 %reduce-scatter.4.cloned.1.call-done = bf16[24,16384]{1,0:T(8,128)(2,1)} async-done(((bf16[192,16384]{1,0:T(8,128)(2,1)}), bf16[24,16384]{1,0:T(8,128)(2,1)}) %reduce-scatter.4.cloned.1.call-update) | async-done | bytes 786448 | tf_op jit(solution)/shard_map/reduce_scatter | solution.py:54
  163.0 1.2 reshape.109
  164.3 0.2 fusion.22
  164.6 2.4 collective-permute-start.1
  167.0 1.3 collective-permute-start
  168.3 18.1 %all_gather.12 = bf16[24,3,2048]{2,0,1:T(8,128)(2,1)S(1)} all-gather(bf16[24,3,256]{2,0,1:T(8,128)(2,1)S(1)} %get-tuple-element.22), channel_id=1, replica_groups=mesh['lev'=8,'gy'=4,'gx'=8] {'gx'}, dimensions={2}, use_global_device_ids=true | all-gather | bytes 331776 | tf_op jit(solution)/shard_map/all_gather | solution.py:66
  186.4 2.5 copy.27
  188.9 10.5 rev.6
  199.3 3.3 gather_fusion.1
  202.8 1.1 fusion.50
  203.9 2.5 collective-permute-start.2
  206.4 0.3 select_bitcast_fusion.1
  206.8 0.8 copy.28
  207.6 8.4 collective-permute-done.2
  216.0 0.7 collective-permute-done.3
  216.8 1.6 pad_maximum_fusion
  218.5 0.6 copy-done.7
  219.5 1.0 maximum_select_fusion
  220.9 15.0 %fusion.48 = (bf16[64,256]{1,0:T(8,128)(2,1)}, bf16[64,256]{1,0:T(8,128)(2,1)}, f32[24,64,256]{2,0,1:T(8,128)S(1)}) fusion(bf16[24,70,262]{2,0,1:T(8,128)(2,1)S(1)} %maximum_select_fusion, f32[24]{0:T(128)S(1)} %copy-done.40, f32[24]{0:T(128)S(1)} %copy-done.41, f32[24]{0:T(128)S(1)} %copy-done.42, f32[24]{0:T(128)S(1)} %copy-done.43, f32[24]{0:T(128)S(1)} %copy-done.44, ...), kind=kLoop, calls=%fused_computation.185 | loop fusion | flops 58556416 | bytes 40178272 | tf_op jit(solution)/shard_map/reduce_sum | solution.py:72
  236.0 96.7 %all-reduce.7.cloned.1.call-done = (bf16[64,256]{1,0:T(8,128)(2,1)}, bf16[64,256]{1,0:T(8,128)(2,1)}) async-done(((bf16[64,256]{1,0:T(8,128)(2,1)}, bf16[64,256]{1,0:T(8,128)(2,1)}), (bf16[64,256]{1,0:T(8,128)(2,1)}, bf16[64,256]{1,0:T(8,128)(2,1)})) %all-reduce.7.cloned.1.call-update) | async-done | bytes 65552 | tf_op jit(solution)/shard_map/psum | solution.py:73
  332.6 0.8 convert_multiply_fusion.1
  333.4 0.5 fusion.23
  333.9 0.9 copy.42
  334.9 134.4 %all-gather.3.cloned.1.call-done = bf16[192,16384]{1,0:T(8,128)(2,1)} async-done(((bf16[24,16384]{1,0:T(8,128)(2,1)}), bf16[192,16384]{1,0:T(8,128)(2,1)}) %all-gather.3.cloned.1.call-update) | async-done | bytes 6291472 | tf_op jit(solution)/shard_map/all_gather | solution.py:83
  469.3 7.6 fusion
  476.9 0.7 copy-done.9
  477.6 152.0 %reduce-scatter.6.cloned.1.call-done = bf16[24,16384]{1,0:T(8,128)(2,1)} async-done(((bf16[192,16384]{1,0:T(8,128)(2,1)}), bf16[24,16384]{1,0:T(8,128)(2,1)}) %reduce-scatter.6.cloned.1.call-update) | async-done | bytes 786448 | tf_op jit(solution)/shard_map/reduce_scatter | solution.py:91
  629.6 1.2 reshape.112
  630.9 0.4 fusion.21
  631.3 2.5 collective-permute-start.5
  633.9 1.3 collective-permute-start.4
  635.2 18.2 %all_gather.14 = bf16[24,3,2048]{2,0,1:T(8,128)(2,1)S(1)} all-gather(bf16[24,3,256]{2,0,1:T(8,128)(2,1)S(1)} %get-tuple-element.20), channel_id=1, replica_groups=mesh['lev'=8,'gy'=4,'gx'=8] {'gx'}, dimensions={2}, use_global_device_ids=true | all-gather | bytes 331776 | tf_op jit(solution)/shard_map/all_gather | solution.py:66
  653.4 2.5 copy.32
  655.9 10.5 rev.7
  666.4 2.6 gather_fusion.2
  669.1 0.2 fusion.49
  669.3 2.6 collective-permute-start.6
  671.9 0.3 select_bitcast_fusion
  672.3 0.2 copy.33
  672.5 8.7 collective-permute-done.6
  681.2 0.8 collective-permute-done.7
  682.0 0.8 pad_maximum_fusion.1
  682.9 0.1 slice.972
  683.0 1.0 maximum_select_fusion.1
  684.0 14.0 %fusion.47 = (bf16[64,256]{1,0:T(8,128)(2,1)}, bf16[64,256]{1,0:T(8,128)(2,1)}, f32[24,64,256]{2,0,1:T(8,128)S(1)}) fusion(bf16[24,70,262]{2,0,1:T(8,128)(2,1)S(1)} %maximum_select_fusion.1, f32[24]{0:T(128)S(1)} %get-tuple-element.31, f32[24]{0:T(128)S(1)} %get-tuple-element.32, f32[24]{0:T(128)S(1)} %get-tuple-element.33, f32[24]{0:T(128)S(1)} %get-tuple-element.34, ...), kind=kLoop, calls=%fused_computation.184 | loop fusion | flops 58556416 | bytes 40178272 | tf_op jit(solution)/shard_map/reduce_sum | solution.py:72
  698.0 96.8 %all-reduce.5.cloned.1.call-done = (bf16[64,256]{1,0:T(8,128)(2,1)}, bf16[64,256]{1,0:T(8,128)(2,1)}) async-done(((bf16[64,256]{1,0:T(8,128)(2,1)}, bf16[64,256]{1,0:T(8,128)(2,1)}), (bf16[64,256]{1,0:T(8,128)(2,1)}, bf16[64,256]{1,0:T(8,128)(2,1)})) %all-reduce.5.cloned.1.call-update) | async-done | bytes 65552 | tf_op jit(solution)/shard_map/psum | solution.py:73
  794.9 0.8 convert_multiply_fusion
  795.7 0.5 fusion.24
  796.2 0.9 copy.43
  797.1 0.3 reduce-scatter.8.cloned.1.call-start
  797.4 133.9 %all-gather.5.cloned.1.call-done = bf16[192,16384]{1,0:T(8,128)(2,1)} async-done(((bf16[24,16384]{1,0:T(8,128)(2,1)}), bf16[192,16384]{1,0:T(8,128)(2,1)}) %all-gather.5.cloned.1.call-update) | async-done | bytes 6291472 | tf_op jit(solution)/shard_map/all_gather | solution.py:83
  931.4 7.6 fusion.1
  939.0 152.3 %reduce-scatter.8.cloned.1.call-done = bf16[24,16384]{1,0:T(8,128)(2,1)} async-done(((bf16[192,16384]{1,0:T(8,128)(2,1)}), bf16[24,16384]{1,0:T(8,128)(2,1)}) %reduce-scatter.8.cloned.1.call-update) | async-done | bytes 786448 | tf_op jit(solution)/shard_map/reduce_scatter | solution.py:91
  1091.3 1.2 reshape.115
  1092.5 0.3 fusion.19
  1092.8 1.1 copy.36
  (140 shorter events, 1.1 us)
Async XLA Ops:
  6.5 2.1 copy-start
  6.5 156.5 %reduce-scatter.4.cloned.1.call-start = ((), (), s32[]{:S(2)}) async-start(), calls=%async_computation.3 | async-start | bytes 7077888 | tf_op jit(solution)/shard_map/reduce_scatter | solution.py:54
  13.1 3.2 copy-start.11
  13.1 319.5 %all-reduce.7.cloned.1.call-start = ((), (), s32[]{:S(2)}) async-start(), calls=%async_computation.9 | async-start | bytes 131072 | tf_op jit(solution)/shard_map/psum | solution.py:73
  13.9 150.4 %copy-start.3 = (f32[64,256]{1,0:T(8,128)}, f32[64,256]{1,0:T(8,128)S(1)}, u32[]{:S(2)}) copy-start(f32[64,256]{1,0:T(8,128)S(1)} %convert_element_type.392) | copy-start | bytes 196612
  164.6 38.1 %collective-permute-start.1 = (bf16[24,3,256]{2,0,1:T(8,128)(2,1)S(1)}, bf16[24,3,256]{2,0,1:T(8,128)(2,1)S(1)}, u32[]{:S(2)}, u32[]{:S(2)}) collective-permute-start(bf16[24,3,256]{2,0,1:T(8,128)(2,1)S(1)} %get-tuple-element.23), channel_id=1, source_target_pairs={{8,0},{16,8},{24,16},{9,1},{17,9},{25,17},{10,2},{18,10},{26,18},{... | collective-permute-start | bytes 110600 | tf_op jit(solution)/shard_map/ppermute | solution.py:19
  167.0 35.7 %collective-permute-start = (bf16[24,3,256]{2,0,1:T(8,128)(2,1)S(1)}, bf16[24,3,256]{2,0,1:T(8,128)(2,1)S(1)}, u32[]{:S(2)}, u32[]{:S(2)}) collective-permute-start(bf16[24,3,256]{2,0,1:T(8,128)(2,1)S(1)} %get-tuple-element.22), channel_id=1, source_target_pairs={{0,8},{8,16},{16,24},{1,9},{9,17},{17,25},{2,10},{10,18},{18,26},{... | collective-permute-start | bytes 110600 | tf_op jit(solution)/shard_map/ppermute | solution.py:17
  202.7 3.8 copy-start.5
  202.7 1.2 copy-start.6
  203.9 12.1 %collective-permute-start.2 = (bf16[24,70,3]{2,0,1:T(8,128)(2,1)}, bf16[24,70,3]{2,0,1:T(8,128)(2,1)S(1)}, u32[]{:S(2)}, u32[]{:S(2)}) collective-permute-start(bf16[24,70,3]{2,0,1:T(8,128)(2,1)} %get-tuple-element.18), channel_id=1, source_target_pairs={{0,1},{1,2},{2,3},{3,4},{4,5},{5,6},{6,7},{7,0},{8,9},{9,10},{10,1... | collective-permute-start | bytes 30248 | tf_op jit(solution)/shard_map/ppermute | solution.py:17
  206.4 10.3 collective-permute-start.3
  219.2 1.4 copy-start.13
  219.2 1.4 copy-start.14
  219.2 1.4 copy-start.15
  219.2 1.4 copy-start.16
  219.2 1.4 copy-start.17
  219.2 1.4 copy-start.18
  219.2 1.4 copy-start.19
  219.2 1.4 copy-start.20
  219.2 1.4 copy-start.21
  219.2 1.4 copy-start.22
  219.2 1.4 copy-start.23
  219.3 1.4 copy-start.24
  219.3 1.4 copy-start.25
  219.3 1.4 copy-start.26
  219.3 1.4 copy-start.27
  219.3 1.4 copy-start.28
  219.3 1.4 copy-start.29
  219.3 1.4 copy-start.30
  219.3 1.4 copy-start.31
  219.3 1.4 copy-start.32
  219.3 1.4 copy-start.33
  219.4 1.4 copy-start.34
  219.4 1.4 copy-start.35
  219.4 1.4 copy-start.36
  219.4 1.4 copy-start.37
  219.4 1.4 copy-start.38
  219.4 1.4 copy-start.39
  219.4 1.4 copy-start.40
  219.4 1.4 copy-start.41
  219.4 1.4 copy-start.42
  219.4 1.4 copy-start.43
  219.5 1.4 copy-start.44
  219.5 1.4 copy-start.45
  219.5 1.4 copy-start.46
  219.5 1.4 copy-start.47
  219.5 1.4 copy-start.48
  219.5 1.4 copy-start.49
  220.9 15.1 %copy-start.12 = (bf16[2,24]{1,0:T(2,128)(2,1)S(1)}, bf16[2,24]{1,0:T(2,128)(2,1)}, u32[]{:S(2)}) copy-start(bf16[2,24]{1,0:T(2,128)(2,1)} %param.15) | copy-start | bytes 292
  235.9 233.4 %all-gather.3.cloned.1.call-start = ((), (), s32[]{:S(2)}) async-start(), calls=%async_computation.4 | async-start | bytes 7077888 | tf_op jit(solution)/shard_map/all_gather | solution.py:83
  333.9 135.4 %copy-start.50 = (bf16[2,96,192]{2,1,0:T(8,128)(2,1)S(1)}, bf16[2,96,192]{2,1,0:T(8,128)(2,1)}, u32[]{:S(2)}) copy-start(bf16[2,96,192]{2,1,0:T(8,128)(2,1)} %param.17) | copy-start | bytes 221188
  333.9 135.4 %copy-start.52 = (bf16[2,96,192]{2,1,0:T(8,128)(2,1)S(1)}, bf16[2,96,192]{2,1,0:T(8,128)(2,1)}, u32[]{:S(2)}) copy-start(bf16[2,96,192]{2,1,0:T(8,128)(2,1)} %param.16) | copy-start | bytes 221188
  334.9 294.8 %reduce-scatter.6.cloned.1.call-start = ((), (), s32[]{:S(2)}) async-start(), calls=%async_computation.5 | async-start | bytes 7077888 | tf_op jit(solution)/shard_map/reduce_scatter | solution.py:91
  476.9 154.0 %copy-start.4 = (f32[64,256]{1,0:T(8,128)S(1)}, f32[64,256]{1,0:T(8,128)}, u32[]{:S(2)}) copy-start(f32[64,256]{1,0:T(8,128)} %copy-done.3) | copy-start | bytes 196612
  476.9 318.0 %all-reduce.5.cloned.1.call-start = ((), (), s32[]{:S(2)}) async-start(), calls=%async_computation.8 | async-start | bytes 131072 | tf_op jit(solution)/shard_map/psum | solution.py:73
  631.3 37.6 %collective-permute-start.5 = (bf16[24,3,256]{2,0,1:T(8,128)(2,1)S(1)}, bf16[24,3,256]{2,0,1:T(8,128)(2,1)S(1)}, u32[]{:S(2)}, u32[]{:S(2)}) collective-permute-start(bf16[24,3,256]{2,0,1:T(8,128)(2,1)S(1)} %get-tuple-element.21), channel_id=1, source_target_pairs={{8,0},{16,8},{24,16},{9,1},{17,9},{25,17},{10,2},{18,10},{26,18},{... | collective-permute-start | bytes 110600 | tf_op jit(solution)/shard_map/ppermute | solution.py:19
  633.9 35.1 %collective-permute-start.4 = (bf16[24,3,256]{2,0,1:T(8,128)(2,1)S(1)}, bf16[24,3,256]{2,0,1:T(8,128)(2,1)S(1)}, u32[]{:S(2)}, u32[]{:S(2)}) collective-permute-start(bf16[24,3,256]{2,0,1:T(8,128)(2,1)S(1)} %get-tuple-element.20), channel_id=1, source_target_pairs={{0,8},{8,16},{16,24},{1,9},{9,17},{17,25},{2,10},{10,18},{18,26},{... | collective-permute-start | bytes 110600 | tf_op jit(solution)/shard_map/ppermute | solution.py:17
  669.3 11.9 %collective-permute-start.6 = (bf16[24,70,3]{2,0,1:T(8,128)(2,1)S(1)}, bf16[24,70,3]{2,0,1:T(8,128)(2,1)S(1)}, u32[]{:S(2)}, u32[]{:S(2)}) collective-permute-start(bf16[24,70,3]{2,0,1:T(8,128)(2,1)S(1)} %get-tuple-element.16), channel_id=1, source_target_pairs={{0,1},{1,2},{2,3},{3,4},{4,5},{5,6},{6,7},{7,0},{8,9},{9,10},{10,1... | collective-permute-start | bytes 30248 | tf_op jit(solution)/shard_map/ppermute | solution.py:17
  671.9 10.1 collective-permute-start.7
  698.0 233.4 %all-gather.5.cloned.1.call-start = ((), (), s32[]{:S(2)}) async-start(), calls=%async_computation.6 | async-start | bytes 7077888 | tf_op jit(solution)/shard_map/all_gather | solution.py:83
  796.2 135.2 %copy-start.51 = (bf16[2,96,192]{2,1,0:T(8,128)(2,1)S(1)}, bf16[2,96,192]{2,1,0:T(8,128)(2,1)}, u32[]{:S(2)}) copy-start(bf16[2,96,192]{2,1,0:T(8,128)(2,1)} %param.17) | copy-start | bytes 221188
  796.2 135.2 %copy-start.53 = (bf16[2,96,192]{2,1,0:T(8,128)(2,1)S(1)}, bf16[2,96,192]{2,1,0:T(8,128)(2,1)}, u32[]{:S(2)}) copy-start(bf16[2,96,192]{2,1,0:T(8,128)(2,1)} %param.16) | copy-start | bytes 221188
  797.1 294.2 %reduce-scatter.8.cloned.1.call-start = ((), (), s32[]{:S(2)}) async-start(), calls=%async_computation.7 | async-start | bytes 7077888 | tf_op jit(solution)/shard_map/reduce_scatter | solution.py:91
  1092.5 1.4 copy-start.1
  (5 other events, 4.1 us)
Sparse Core Ops, SparseCore 0:
  13.2 149.7 reduce-scatter.3
  236.0 96.5 all-reduce.6
  335.2 134.0 all-gather.2
  477.0 152.5 reduce-scatter.5
  698.1 96.7 all-reduce.4
  797.3 134.0 all-gather.4
  939.1 152.1 reduce-scatter.7
where the time goes:
time: 1110 us; the launch traced here: 1100 us
  waiting for transfers between devices  929 us (84%)
  local copies, waits for them, and re-layouts  46.6 us (4%)
  other arithmetic  41.6 us (4%)
  blocking collectives  36.3 us (3%)
  matrix products  19.6 us (2%)
  between operations  14.5 us (1%)
  starting transfers between devices  13.1 us (1%)
    reduce_scatter x2, waiting for transfers between devices, body(): lax.psum_scatter(rounded(part).astype(jnp.bfloat16), 'lev', scatter_dimen...  304 us
    all_gather x2, waiting for transfers between devices, body(): lax.all_gather(normed.reshape(chan_local, cells), 'lev', axis=0, tiled=True)  268 us
    psum x2, waiting for transfers between devices, body(): lax.psum(jnp.sum(conv * conv, axis=0).astype(jnp.bfloat16), 'lev')  193 us
    reduce_scatter x1, waiting for transfers between devices, body(): lax.psum_scatter(rounded(stem_part).astype(jnp.bfloat16), 'lev', scatter_...  144 us
    all_gather x2, blocking collectives, body(): whole_rim = lax.all_gather(rim, 'gx', axis=2, tiled=True)  36.3 us
    reduce_sum x2, other arithmetic, body(): jnp.sum(conv, axis=0).astype(jnp.bfloat16)  28.9 us
  transfers between devices with their start and end apart: 15, of which 11 were waited for; matrix products, arithmetic and copies ran while one was open for 3% of the time, Pallas kernels for 0%

commit v1 on v0

v1 whole, which is shorter than its diff:
```python
import jax
import jax.numpy as jnp
from jax import lax
from jax.experimental import pallas as pl
from jax.experimental.pallas import tpu as pltpu
from jax.sharding import PartitionSpec as P

BF = jnp.bfloat16
F32 = jnp.float32
MESH = pl.DeviceIdType.MESH
GROUPS = 12


def device(x, y, z, c):
    return (y * 2 + z // 4, x, lax.rem(z, 4) * 2 + c)


def kernel(
    fields, sea, partner, embed, dwg, up, down,
    out,
    x_in, mask_in, xt, flat, pe, dw_in, dw_all, emb_t, w_own, w_other, down_t, gain, conv,
    state, south, north, pack_e, pack_w, from_w, from_e, xrow, srow,
    fold_in, fold_out, out_f, out_b,
    s_x, r_x, s_m, r_m, s_loc, s_w, r_w, s_halo, r_halo, s_f1, r_f1, s_f3, r_f3, s_o, r_o,
):
    lev = lax.axis_index("lev")
    x = lax.axis_index("gy")
    gx = lax.axis_index("gx")
    y = lev // 2
    z = lax.rem(lev, 2) * 4 + gx // 2
    c = lax.rem(gx, 2)

    def row_block(yy):
        return jnp.where(lax.rem(x, 2) == 0, yy, 3 - yy)

    def is_b(zz):
        return jnp.where((zz >= 2) & (zz <= 5), 0, 1)

    def half(zz):
        return lax.rem(is_b(zz) + c, 2)

    def hop(zz, k):
        return lax.rem(zz + k + 8, 8)

    rb = row_block(y)
    b_side = is_b(z)
    s = half(z)
    t = lax.rem(z + 2, 4)
    col_block = (t * 2 + c) * 2 + s
    line = z * 2 + c
    on_line = (x == 3) & (rb == 3)
    has_south = jnp.logical_not((x == 0) & (rb == 0))
    has_north = jnp.logical_not(on_line)

    far = hop(z, 4)
    same_chip = b_side == 1
    east_z = jnp.where(b_side == 0, jnp.where(c == 0, far, 2 + lax.rem(t + 1, 4)), jnp.where(c == 0, z, far))
    east_c = jnp.where(b_side == 0, 0, 1)
    west_z = jnp.where(b_side == 0, jnp.where(c == 1, far, 2 + lax.rem(t + 3, 4)), jnp.where(c == 1, z, far))
    west_c = jnp.where(b_side == 0, 1, 0)
    east = device(x, y, east_z, east_c)
    west = device(x, y, west_z, west_c)
    x_even = lax.rem(x, 2) == 0
    step = jnp.where(x_even, 1, -1)
    north_x = jnp.where(rb == 3, jnp.minimum(x + 1, 3), x)
    north_y = jnp.where(rb == 3, y, jnp.clip(y + step, 0, 3))
    south_x = jnp.where(rb == 0, jnp.maximum(x - 1, 0), x)
    south_y = jnp.where(rb == 0, y, jnp.clip(y - step, 0, 3))
    north_dev = device(north_x, north_y, z, c)
    south_dev = device(south_x, south_y, z, c)

    def remote(src, dst, send, recv, dev):
        return pltpu.make_async_remote_copy(
            src_ref=src, dst_ref=dst, send_sem=send, recv_sem=recv, device_id=dev, device_id_type=MESH
        )

    ys = [lax.rem(y + k, 4) for k in range(4)]

    barrier = pltpu.get_barrier_semaphore()
    peers = [device(x, yy, hop(z, d), c) for d in (2, -2) for yy in ys]
    peers += [device(x, yy, z, c) for yy in ys[1:]]
    peers += [device(x, y, far, c)]
    peers += [device(lax.rem(x + k, 4), y, z, c) for k in (1, 2, 3)]
    peers += [device(x, y, z, 1 - c)]

    def greet(dev):
        pl.semaphore_signal(barrier, inc=1, device_id=dev, device_id_type=MESH)

    for dev in peers:
        greet(dev)

    @pl.when(on_line)
    def _():
        for k in range(1, 8):
            greet(device(x, y, hop(z, k), 1 - c))
            if k % 2:
                greet(device(x, y, hop(z, k), c))

    @pl.when(has_north & (b_side == 0))
    def _():
        greet(device(x, y, jnp.where(c == 0, west_z, east_z), 1 - c))

    slot = pe.at[y, lax.rem(lev, 2)]
    dslot = dw_in.at[y, lax.rem(lev, 2)]
    half_rows = pl.ds(pl.multiple_of(c * 48, 16), 48)
    for k, ref in enumerate((up.at[0], down.at[0], up.at[1], down.at[1])):
        @pl.when(x == k)
        def _():
            pltpu.make_async_copy(ref.at[half_rows, :], slot.at[0], s_loc.at[0]).start()
    pltpu.make_async_copy(embed, slot.at[1], s_loc.at[1]).start()
    pltpu.make_async_copy(dwg, dslot, s_loc.at[2]).start()

    pl.semaphore_wait(barrier, len(peers) + jnp.where(on_line, 11, 1 - b_side))

    pltpu.make_async_copy(up.at[0].at[half_rows, :], slot.at[0], s_loc.at[0]).wait()
    pltpu.make_async_copy(embed, slot.at[1], s_loc.at[1]).wait()
    pltpu.make_async_copy(dwg, dslot, s_loc.at[2]).wait()

    far_dev = device(x, y, far, c)
    w1 = remote(slot, slot, s_w.at[0], r_w.at[0], far_dev)
    w1.start()
    d1 = remote(dslot, dslot, s_w.at[1], r_w.at[1], far_dev)
    d1.start()

    def cells_of(yy, zz):
        return (
            pl.ds(pl.multiple_of(row_block(yy) * 16, 16), 16),
            pl.ds(pl.multiple_of(half(zz) * 128, 128), 128),
        )

    sends = []
    z_up = hop(z, 2)
    mrows, mcols = cells_of(y, z_up)
    m_copy = remote(sea.at[mrows, mcols], mask_in, s_m, r_m, device(x, y, z_up, c))
    m_copy.start()
    for k, yy in enumerate(ys):
        for j, d in enumerate((2, -2)):
            zz = hop(z, d)
            rows, cols = cells_of(yy, zz)
            cp = remote(
                fields.at[:, rows, cols], x_in.at[lev], s_x.at[2 * k + j], r_x.at[lev], device(x, yy, zz, c)
            )
            cp.start()
            sends.append(cp)

    def arrived(dst, sem):
        remote(dst, dst, s_m, sem, far_dev).wait_recv()

    arrived(pe.at[y, 1 - lax.rem(lev, 2)], r_w.at[0])
    arrived(dw_in.at[y, 1 - lax.rem(lev, 2)], r_w.at[1])
    for k in (1, 2, 3):
        dev = device(x, ys[k], z, c)
        cp = remote(pe.at[y], pe.at[y], s_w.at[2 * k], r_w.at[2 + y], dev)
        cp.start()
        sends.append(cp)
        cp = remote(dw_in.at[y], dw_in.at[y], s_w.at[2 * k + 1], r_w.at[6 + y], dev)
        cp.start()
        sends.append(cp)
    for k in (1, 2, 3):
        arrived(pe.at[ys[k]], r_w.at[2 + ys[k]])
        arrived(dw_in.at[ys[k]], r_w.at[6 + ys[k]])

    for k in (1, 2, 3):
        cp = remote(
            pe.at[:, :, 0], w_own.at[x], s_w.at[7 + k], r_w.at[10 + x], device(lax.rem(x + k, 4), y, z, c)
        )
        cp.start()
        sends.append(cp)
    w_own[x] = pe[:, :, 0]
    for l in range(8):
        for b in range(2):
            dw_all[b, l * 24 : (l + 1) * 24, :] = dw_in[l // 2, l % 2, b]
    for b in range(2):
        gain[b] = jnp.broadcast_to(dw_all[b, :, 49:50], (192, 128))
    emb_t[...] = pe[:, :, 1].reshape(384, 192).astype(F32).T.astype(BF)
    for k in (1, 2, 3):
        xk = lax.rem(x + k, 4)
        arrived(w_own.at[xk], r_w.at[10 + xk])
    cp = remote(w_own, w_other, s_w.at[11], r_w.at[14], device(x, y, z, 1 - c))
    cp.start()
    sends.append(cp)

    for k in range(4):
        for d in (2, -2):
            src = ys[k] * 2 + hop(z, d) // 4
            arrived(x_in.at[src], r_x.at[src])
            flat[...] = x_in[src].astype(F32).reshape(640, 128)
            place = pl.ds(pl.multiple_of(src * 48, 16), 48)

            @pl.loop(0, 16)
            def _(r):
                part = flat[pl.ds(r, 40, stride=16), :]
                xt[r, place, :] = jnp.concatenate([part, jnp.zeros((8, 128), F32)], axis=0).astype(BF)

    arrived(mask_in, r_m)

    def sea_rows(r):
        return mask_in[pl.ds(r, 1), :].astype(F32)

    @pl.loop(0, 8)
    def _(i):
        both = jnp.concatenate([xt[2 * i], xt[2 * i + 1]], axis=1)
        stem = jnp.dot(emb_t[...], both, preferred_element_type=F32)
        state[0, 2 * i] = (stem[:, :128] * sea_rows(2 * i)).astype(BF)
        state[0, 2 * i + 1] = (stem[:, 128:] * sea_rows(2 * i + 1)).astype(BF)

    lane = lax.broadcasted_iota(jnp.int32, (16, 128), 1)

    def fold(b):
        for p in range(GROUPS):
            chans = pl.ds(p * 16, 16)

            @pl.when(line == p)
            def _():
                fold_in[b, col_block] = state[b, 13:16, p * 16 : (p + 1) * 16, :]

            @pl.when(line != p)
            def _():
                remote(
                    state.at[b, pl.ds(13, 3), chans, :], fold_in.at[b, col_block],
                    s_f1.at[b, p], r_f1.at[b, col_block], device(x, y, p // 2, p % 2),
                ).start()

        @pl.when(line < GROUPS)
        def _():
            for k in range(1, 16):
                j = lax.rem(col_block + k, 16)
                arrived(fold_in.at[b, j], r_f1.at[b, j])
            rim = jnp.concatenate([fold_in[b, j].reshape(48, 128) for j in range(16)], axis=1)
            column = lax.broadcasted_iota(jnp.int32, (2048, 128), 0)

            @pl.loop(0, 16)
            def _(j):
                onehot = jnp.where(column == partner[pl.ds(j, 1), :], 1.0, 0.0).astype(BF)
                got = jnp.dot(rim, onehot, preferred_element_type=F32).astype(BF)
                for k in range(3):
                    fold_out[b, j, k] = got[(2 - k) * 16 : (3 - k) * 16, :]

            chans = pl.ds(pl.multiple_of(line * 16, 16), 16)
            for j in range(16):
                tj, cj, sj = j // 4, (j // 2) % 2, j % 2
                zj = (tj + 2 + 4 * (sj ^ cj)) % 8

                @pl.when(col_block == j)
                def _():
                    north[b, :, chans, :] = fold_out[b, j]

                @pl.when(col_block != j)
                def _():
                    remote(
                        fold_out.at[b, j], north.at[b, :, chans, :],
                        s_f3.at[b, j], r_f3.at[b, line], device(x, y, zj, cj),
                    ).start()

        for p in range(GROUPS):
            @pl.when(line != p)
            def _():
                arrived(north.at[b, :, pl.ds(p * 16, 16), :], r_f3.at[b, p])

    def fold_sent(b):
        for p in range(GROUPS):
            @pl.when(line != p)
            def _():
                remote(
                    state.at[b, pl.ds(13, 3), pl.ds(p * 16, 16), :], fold_in.at[b, col_block],
                    s_f1.at[b, p], r_f1.at[b, 0], far_dev,
                ).wait_send()

        @pl.when(line < GROUPS)
        def _():
            for j in range(16):
                @pl.when(col_block != j)
                def _():
                    remote(
                        fold_out.at[b, j], fold_out.at[b, j], s_f3.at[b, j], r_f3.at[b, 0], far_dev
                    ).wait_send()

    def halo(b):
        to_north = remote(
            state.at[b, pl.ds(13, 3)], south.at[b], s_halo.at[b, 0], r_halo.at[b, 0], north_dev
        )
        to_south = remote(
            state.at[b, pl.ds(0, 3)], north.at[b], s_halo.at[b, 1], r_halo.at[b, 1], south_dev
        )

        @pl.when(has_north)
        def _():
            to_north.start()

        @pl.when(has_south)
        def _():
            to_south.start()

        @pl.when(on_line)
        def _():
            fold(b)

        @pl.when(has_south)
        def _():
            arrived(south.at[b], r_halo.at[b, 0])

        @pl.when(jnp.logical_not(has_south))
        def _():
            south[b] = jnp.zeros((3, 192, 128), BF)

        @pl.when(has_north)
        def _():
            arrived(north.at[b], r_halo.at[b, 1])

        @pl.loop(0, GROUPS)
        def _(g):
            ch = pl.ds(pl.multiple_of(g * 16, 16), 16)
            to_e = jnp.zeros((16, 128), F32)
            to_w = jnp.zeros((16, 128), F32)
            for r in range(22):
                v = padded_row(b, r, ch)
                here = (lane >= 3 * r) & (lane < 3 * r + 3)
                to_e = jnp.where(here, pltpu.roll(v, (3 * r - 125) % 128, 1), to_e)
                to_w = jnp.where(here, pltpu.roll(v, 3 * r, 1) if r else v, to_w)
            pack_e[b, ch, :] = to_e.astype(BF)
            pack_w[b, ch, :] = to_w.astype(BF)

        go_e = remote(pack_e.at[b], from_w.at[b], s_halo.at[b, 2], r_halo.at[b, 2], east)
        go_w = remote(pack_w.at[b], from_e.at[b], s_halo.at[b, 3], r_halo.at[b, 3], west)
        go_e.start()
        go_w.start()
        sends.append(go_e)
        sends.append(go_w)
        arrived(from_w.at[b], r_halo.at[b, 2])
        arrived(from_e.at[b], r_halo.at[b, 3])
        return to_north, to_south

    def padded_row(b, r, ch):
        if r < 3:
            v = south[b, r, ch, :]
        elif r < 19:
            v = state[b, r - 3, ch, :]
        else:
            v = north[b, r - 19, ch, :]
        return v.astype(F32)

    def depthwise(b):
        @pl.loop(0, GROUPS)
        def _(g):
            ch = pl.ds(pl.multiple_of(g * 16, 16), 16)
            fw = from_w[b, ch, :].astype(F32)
            fe = from_e[b, ch, :].astype(F32)
            for r in range(22):
                xrow[r] = padded_row(b, r, ch)
                left = pltpu.roll(fw, (125 - 3 * r) % 128, 1)
                right = pltpu.roll(fe, (-3 * r) % 128, 1) if r else fe
                srow[r] = jnp.where(lane < 64, right, left)
            taps = dw_all[b, ch, :]
            acc = [None] * 16
            for e in range(7):
                w = [jnp.broadcast_to(taps[:, a * 7 + e : a * 7 + e + 1], (16, 128)) for a in range(7)]
                o = e - 3
                for r in range(22):
                    v = xrow[r]
                    if o < 0:
                        v = pltpu.roll(jnp.where(lane >= 128 + o, srow[r], v), -o, 1)
                    elif o > 0:
                        v = pltpu.roll(jnp.where(lane < o, srow[r], v), 128 - o, 1)
                    for a in range(7):
                        q = r - a
                        if 0 <= q < 16:
                            term = w[a] * v
                            acc[q] = term if acc[q] is None else acc[q] + term
            for q in range(16):
                conv[q, ch, :] = acc[q]

    def pointwise(b):
        down_t[0] = w_own[2 * b + 1].reshape(384, 192).astype(F32).T.astype(BF)
        down_t[1] = w_other[2 * b + 1].reshape(384, 192).astype(F32).T.astype(BF)

        @pl.loop(0, 8)
        def _(i):
            parts = []
            for k in range(2):
                cv = conv[2 * i + k]
                mu = jnp.sum(cv, axis=0, keepdims=True) * (1.0 / 192)
                var = jnp.sum(cv * cv, axis=0, keepdims=True) * (1.0 / 192) - mu * mu
                parts.append(((cv - mu) * lax.rsqrt(var + 1e-6) * gain[b]).astype(BF))
            normed = jnp.concatenate(parts, axis=1)
            branch = jnp.zeros((192, 256), F32)
            for side, w in enumerate((w_own, w_other)):
                pre = jnp.dot(w[2 * b].reshape(384, 192), normed, preferred_element_type=F32)
                hidden = jax.nn.gelu(pre, approximate=True).astype(BF)
                branch = branch + jnp.dot(down_t[side], hidden, preferred_element_type=F32)
            for k in range(2):
                r = 2 * i + k
                new = (state[b, r].astype(F32) + branch[:, k * 128 : (k + 1) * 128]) * sea_rows(r)
                if b == 0:
                    state[1, r] = new.astype(BF)
                else:
                    out_f[pl.ds(r, 192, stride=16), :] = new

    pairs = []
    for b in range(2):
        pairs.append(halo(b))
        depthwise(b)
        if b == 0:
            arrived(w_other, r_w.at[14])
        pointwise(b)

    my_cells = (pl.ds(pl.multiple_of(rb * 16, 16), 16), pl.ds(pl.multiple_of(s * 128, 128), 128))
    for k, yy in enumerate(ys):
        for j, d in enumerate((2, -2)):
            zz = hop(z, d)
            l = yy * 2 + zz // 4
            chans = pl.ds(l * 24, 24)
            out_b[chans] = out_f[pl.ds(pl.multiple_of(l * 384, 384), 384), :].reshape(24, 16, 128).astype(BF)
            cp = remote(
                out_b.at[chans], out.at[:, my_cells[0], my_cells[1]],
                s_o.at[2 * k + j], r_o.at[y * 2 + j], device(x, yy, zz, c),
            )
            cp.start()
            sends.append(cp)
    for k, yy in enumerate(ys):
        for j, d in enumerate((-2, 2)):
            rows, cols = cells_of(yy, hop(z, d))
            arrived(out.at[:, rows, cols], r_o.at[yy * 2 + j])

    w1.wait_send()
    d1.wait_send()
    m_copy.wait_send()
    for cp in sends:
        cp.wait_send()
    for b in range(2):
        to_north, to_south = pairs[b]

        @pl.when(has_north)
        def _():
            to_north.wait_send()

        @pl.when(has_south)
        def _():
            to_south.wait_send()

        @pl.when(on_line)
        def _():
            fold_sent(b)


def body(fields, sea_mask, fold_partner, embed_weight, dw_weight, ln_gain, up_weight, down_weight):
    embed = jnp.pad(embed_weight, ((0, 8), (0, 0)))
    dwg = jnp.concatenate(
        [dw_weight.reshape(2, 24, 49), ln_gain.astype(F32)[:, :, None], jnp.zeros((2, 24, 78), F32)], axis=2
    )
    partner = fold_partner.reshape(16, 128)
    hbm = pl.BlockSpec(memory_space=pl.ANY)
    vmem = pl.BlockSpec(memory_space=pltpu.VMEM)
    dma = pltpu.SemaphoreType.DMA
    scratch = [
        pltpu.VMEM((8, 40, 16, 128), BF),
        pltpu.VMEM((16, 128), jnp.int32),
        pltpu.VMEM((16, 384, 128), BF),
        pltpu.VMEM((640, 128), F32),
        pltpu.VMEM((4, 2, 2, 48, 192), BF),
        pltpu.VMEM((4, 2, 2, 24, 128), F32),
        pltpu.VMEM((2, 192, 128), F32),
        pltpu.VMEM((192, 384), BF),
        pltpu.VMEM((4, 4, 2, 48, 192), BF),
        pltpu.VMEM((4, 4, 2, 48, 192), BF),
        pltpu.VMEM((2, 192, 384), BF),
        pltpu.VMEM((2, 192, 128), F32),
        pltpu.VMEM((16, 192, 128), F32),
        pltpu.VMEM((2, 16, 192, 128), BF),
        pltpu.VMEM((2, 3, 192, 128), BF),
        pltpu.VMEM((2, 3, 192, 128), BF),
        pltpu.VMEM((2, 192, 128), BF),
        pltpu.VMEM((2, 192, 128), BF),
        pltpu.VMEM((2, 192, 128), BF),
        pltpu.VMEM((2, 192, 128), BF),
        pltpu.VMEM((22, 16, 128), F32),
        pltpu.VMEM((22, 16, 128), F32),
        pltpu.VMEM((2, 16, 3, 16, 128), BF),
        pltpu.VMEM((2, 16, 3, 16, 128), BF),
        pltpu.VMEM((192 * 16, 128), F32),
        pltpu.VMEM((192, 16, 128), BF),
        dma((8,)), dma((8,)),
        dma, dma,
        dma((3,)),
        dma((12,)), dma((15,)),
        dma((2, 4)), dma((2, 4)),
        dma((2, 12)), dma((2, 16)),
        dma((2, 16)), dma((2, 12)),
        dma((8,)), dma((8,)),
    ]
    return pl.pallas_call(
        kernel,
        out_shape=jax.ShapeDtypeStruct((24, 64, 256), BF),
        in_specs=[hbm, hbm, vmem, hbm, hbm, hbm, hbm],
        out_specs=hbm,
        scratch_shapes=scratch,
        compiler_params=pltpu.CompilerParams(
            collective_id=0, has_side_effects=True, vmem_limit_bytes=48 * 1024 * 1024
        ),
    )(fields, sea_mask, partner, embed, dwg, up_weight, down_weight)


def solution(mesh):
    in_specs = (
        P("lev", "gy", "gx"),
        P("gy", "gx"),
        P(),
        P("lev", None),
        P(None, "lev", None, None),
        P(None, "lev"),
        P(None, "lev", None),
        P(None, "lev", None),
    )
    out_specs = P("lev", "gy", "gx")
    return jax.shard_map(body, mesh=mesh, in_specs=in_specs, out_specs=out_specs, check_vma=False)
```

time: 1110 us -> 153 us (0.14)
  waiting for transfers between devices: 929 us -> 0 us
  Pallas kernels: 0 us -> 144 us
  other arithmetic: 41.6 us -> 0.73 us
  local copies, waits for them, and re-layouts: 46.6 us -> 7.3 us
  blocking collectives: 36.3 us -> 0 us
  matrix products: 19.6 us -> 0 us
  between operations: 14.5 us -> 0.02 us
  starting transfers between devices: 13.1 us -> 0 us
    reduce_scatter x3 -> x0, waiting for transfers between devices: 448 us -> none  [the longest x2 304 us: body(): lax.psum_scatter(rounded(part).astype(jnp.bfloat16), 'lev', scatter_dimen...]
    all_gather x2 -> x0, waiting for transfers between devices: 268 us -> none  [body(): lax.all_gather(normed.reshape(chan_local, cells), 'lev', axis=0, tiled=True)]
    psum x2 -> x0, waiting for transfers between devices: 193 us -> none  [body(): lax.psum(jnp.sum(conv * conv, axis=0).astype(jnp.bfloat16), 'lev')]
    pallas_call x0 -> x1, Pallas kernels: none -> 144 us  [body(): pl.pallas_call(kernel, out_shape=jax.ShapeDtypeStruct((24, 64, 256), BF),...]
    all_gather x2 -> x0, blocking collectives: 36.3 us -> none  [body(): whole_rim = lax.all_gather(rim, 'gx', axis=2, tiled=True)]
    reduce_sum x2 -> x0, other arithmetic: 28.9 us -> none  [body(): jnp.sum(conv, axis=0).astype(jnp.bfloat16)]
    rev x2 -> x0, local copies, waits for them, and re-layouts: 21 us -> none  [body(): fold_rows = jnp.take(whole_rim[:, ::-1, :], fold_cols, axis=2)]
    dot_general x3 -> x0, matrix products: 19.6 us -> none  [the longest x2 15.1 us: body(): lax.dot_general(down_local, hidden, (((0,), (0,)), ((), ())), preferred_e...]
  transfers between devices with their start and end apart: 15 -> 0, of which waited for: 11 -> 0; matrix products, arithmetic and copies ran while one was open for 3% -> 0% of each run, Pallas kernels for 0% -> 0%
where the time goes in v1:
time: 153 us; the launch traced here: 152 us
  Pallas kernels  144 us (94%)
  local copies, waits for them, and re-layouts  7.3 us (5%)
    pallas_call x1, Pallas kernels, body(): pl.pallas_call(kernel, out_shape=jax.ShapeDtypeStruct((24, 64, 256), BF),...  144 us
    unnamed x11, local copies, waits for them, and re-layouts  5.52 us

profile of v1, /device:TPU:127, one launch (start us, length us, event | category | flops | bytes accessed | tf_op | source)
XLA Modules:
  0.0 152.3 jit_solution(388528280288838962)
XLA Ops:
  0.0 0.1 pad.7.clone
  0.1 0.7 bitcast_convert_fusion
  0.7 0.1 copy.12
  0.8 0.7 pad.4.embed
  1.6 0.9 copy.11
  2.4 0.1 maximum_maximum_fusion.dwg
  2.5 0.0 copy-start
  2.5 1.3 copy-done
  3.8 0.0 copy-start.1
  3.8 0.9 copy-done.1
  4.7 0.0 copy-start.2
  4.7 0.9 copy-done.2
  5.6 0.0 copy-start.3
  5.6 0.8 copy-done.3
  6.5 0.0 copy-start.4
  6.5 0.7 copy-done.4
  7.2 144.3 %shard_map.82 = bf16[24,64,256]{2,1,0:T(8,128)(2,1)S(1)} custom-call(bf16[40,64,256]{2,1,0:T(8,128)(2,1)S(1)} %copy-done, s32[64,256]{1,0:T(8,128)S(1)} %copy-done.3, s32[16,128]{1,0:T(8,128)S(1)} %bitcast.5, bf16[48,192]{1,0:T(8,128)(2,1)S(1)} %pad.4.embed, f32[2,24,128]{2,1,0:T(8,128)S(1)} %maximum_maximum_fusion.dwg, bf16[2,96,192]{2,1,0:T(8,128)(2,1)S(1)} %copy-done.1, ...), custom_call_target="tpu_custom_call" | custom-call | tf_op jit(solution)/shard_map/pallas_call | solution.py:490
  151.5 0.9 copy.14
  (1 shorter events, 0.0 us)
Async XLA Ops:
  2.5 1.3 copy-start
  3.8 0.9 copy-start.1
  4.7 0.9 copy-start.2
  5.6 0.8 copy-start.3
  6.5 0.7 copy-start.4

commit v2 on v0

v2 whole, which is shorter than its diff:
```python
import jax
import jax.numpy as jnp
from jax import lax
from jax.experimental import pallas as pl
from jax.experimental.pallas import tpu as pltpu
from jax.sharding import PartitionSpec as P

BF = jnp.bfloat16
F32 = jnp.float32
MESH = pl.DeviceIdType.MESH
GROUPS = 12


def kernel(
    fields, sea, partner, embed, dw_weight, ln_gain, up, down,
    out,
    x_in, sea_in, partner_in, embed_in, dw_raw, gain_raw,
    xt, flat, pe, dw_in, dw_all, emb_t, w_own, w_other, down_t, gain, conv,
    state, south, north, sides, sides_s, sides_n, pack_e, pack_w, from_w, from_e, xrow, srow,
    onehot, fold_in, fold_out, out_f, out_b,
    s_x, r_x, s_loc, s_w, r_w, s_halo, r_halo, s_f1, r_f1, s_f3, r_f3, s_o, r_o,
):
    lev = lax.axis_index("lev")
    x = lax.axis_index("gy")
    gx = lax.axis_index("gx")
    y = lev // 2
    h = lax.rem(lev, 2)
    t = gx // 2
    c = lax.rem(gx, 2)

    def row_block(yy):
        return jnp.where(lax.rem(x, 2) == 0, yy, 3 - yy)

    def half(hh):
        return lax.rem(hh + c, 2)

    def device(xx, yy, hh, tt, cc):
        return (yy * 2 + hh, xx, tt * 2 + cc)

    rb = row_block(y)
    s = half(h)
    col_block = (t * 2 + c) * 2 + s
    line = gx * 2 + h
    on_line = (x == 3) & (rb == 3)
    has_south = jnp.logical_not((x == 0) & (rb == 0))
    has_north = jnp.logical_not(on_line)

    outer_t = lax.rem(t + jnp.where(c == 0, 3, 1), 4)
    far = device(x, y, 1 - h, t, c)
    near = device(x, y, h, jnp.where(h == 0, outer_t, t), 1 - c)
    east_far = h == c
    east = tuple(jnp.where(east_far, f, n) for f, n in zip(far, near))
    west = tuple(jnp.where(east_far, n, f) for f, n in zip(far, near))
    step = jnp.where(lax.rem(x, 2) == 0, 1, -1)
    north_dev = device(
        jnp.where(rb == 3, jnp.minimum(x + 1, 3), x), jnp.where(rb == 3, y, jnp.clip(y + step, 0, 3)), h, t, c
    )
    south_dev = device(
        jnp.where(rb == 0, jnp.maximum(x - 1, 0), x), jnp.where(rb == 0, y, jnp.clip(y - step, 0, 3)), h, t, c
    )

    def remote(src, dst, send, recv, dev):
        return pltpu.make_async_remote_copy(
            src_ref=src, dst_ref=dst, send_sem=send, recv_sem=recv, device_id=dev, device_id_type=MESH
        )

    def arrived(dst, sem):
        remote(dst, dst, s_w.at[0], sem, far).wait_recv()

    ys = [lax.rem(y + k, 4) for k in range(4)]

    def cells_of(yy, hh):
        return (
            pl.ds(pl.multiple_of(row_block(yy) * 16, 16), 16),
            pl.ds(pl.multiple_of(half(hh) * 128, 128), 128),
        )

    my_rows, my_cols = cells_of(y, h)

    half_rows = pl.ds(pl.multiple_of(c * 48, 16), 48)
    slot = pe.at[y, h]
    dslot = dw_in.at[y, h]
    for k, ref in enumerate((up.at[0], down.at[0], up.at[1], down.at[1])):
        @pl.when(x == k)
        def _():
            pltpu.make_async_copy(ref.at[half_rows, :], slot.at[0], s_loc.at[0]).start()
    own = [
        pltpu.make_async_copy(embed, embed_in, s_loc.at[1]),
        pltpu.make_async_copy(dw_weight, dw_raw, s_loc.at[2]),
        pltpu.make_async_copy(ln_gain, gain_raw, s_loc.at[3]),
        pltpu.make_async_copy(sea.at[my_rows, my_cols], sea_in, s_loc.at[4]),
        pltpu.make_async_copy(partner, partner_in, s_loc.at[5]),
        pltpu.make_async_copy(fields.at[:, my_rows, my_cols], x_in.at[lev], s_loc.at[6]),
    ]
    for cp in own:
        cp.start()

    barrier = pltpu.get_barrier_semaphore()
    peers = [device(x, yy, 1 - h, t, c) for yy in ys]
    peers += [device(x, yy, h, t, c) for yy in ys[1:]]
    peers += [device(lax.rem(x + k, 4), y, h, t, c) for k in (1, 2, 3)]
    peers += [device(x, y, h, t, 1 - c)]

    def greet(dev):
        pl.semaphore_signal(barrier, inc=1, device_id=dev, device_id_type=MESH)

    for dev in peers:
        greet(dev)

    @pl.when(on_line)
    def _():
        for k in (1, 2, 3):
            for hh in range(2):
                for cc in range(2):
                    greet(device(x, y, hh, lax.rem(t + k, 4), cc))
        greet(device(x, y, 1 - h, t, 1 - c))

    @pl.when(has_north & (h == 0))
    def _():
        greet(near)

    own[0].wait()
    own[1].wait()
    own[2].wait()
    slot[1] = jnp.concatenate([embed_in[...].astype(F32), jnp.zeros((8, 192), F32)], axis=0).astype(BF)
    diagonal = lax.broadcasted_iota(jnp.int32, (24, 24), 0) == lax.broadcasted_iota(jnp.int32, (24, 24), 1)
    gains = gain_raw[...].astype(F32)
    for b in range(2):
        raw = dw_raw[b]
        column = jnp.sum(jnp.where(diagonal, gains[b : b + 1, :], 0.0), axis=1, keepdims=True)
        dslot[b] = jnp.concatenate(
            [raw[:, a, :] for a in range(7)] + [column, jnp.zeros((24, 78), F32)], axis=1
        )
    pltpu.make_async_copy(up.at[0].at[half_rows, :], slot.at[0], s_loc.at[0]).wait()

    pl.semaphore_wait(barrier, len(peers) + jnp.where(on_line, 13, 1 - h))

    sends = []

    def send(src, dst, send_sem, recv_sem, dev):
        cp = remote(src, dst, send_sem, recv_sem, dev)
        cp.start()
        sends.append(cp)

    send(slot, slot, s_w.at[0], r_w.at[0], far)
    send(dslot, dslot, s_w.at[1], r_w.at[1], far)

    others = [(k, 1) for k in range(4)] + [(k, 0) for k in range(1, 4)]
    for i, (k, flip) in enumerate(others):
        hh = lax.rem(h + flip, 2)
        rows, cols = cells_of(ys[k], hh)
        send(
            fields.at[:, rows, cols], x_in.at[lev], s_x.at[i], r_x.at[lev], device(x, ys[k], hh, t, c)
        )

    arrived(pe.at[y, 1 - h], r_w.at[0])
    arrived(dw_in.at[y, 1 - h], r_w.at[1])
    for k in (1, 2, 3):
        dev = device(x, ys[k], h, t, c)
        send(pe.at[y], pe.at[y], s_w.at[2 * k], r_w.at[2 + y], dev)
        send(dw_in.at[y], dw_in.at[y], s_w.at[2 * k + 1], r_w.at[6 + y], dev)

    own[4].wait()

    @pl.when(on_line & (line < GROUPS))
    def _():
        @pl.loop(0, 8)
        def _(j):
            @pl.loop(0, 16)
            def _(m):
                source = lax.broadcasted_iota(jnp.int32, (128, 128), 0) + m * 128
                for q in range(2):
                    hit = source == partner_in[pl.ds(2 * j + q, 1), :]
                    onehot[j, pl.ds(pl.multiple_of(m * 128, 128), 128), q * 128 : (q + 1) * 128] = jnp.where(
                        hit, 1.0, 0.0
                    ).astype(BF)

    for k in (1, 2, 3):
        arrived(pe.at[ys[k]], r_w.at[2 + ys[k]])
        arrived(dw_in.at[ys[k]], r_w.at[6 + ys[k]])

    for k in (1, 2, 3):
        send(
            pe.at[:, :, 0], w_own.at[x], s_w.at[7 + k], r_w.at[10 + x], device(lax.rem(x + k, 4), y, h, t, c)
        )
    w_own[x] = pe[:, :, 0]
    for l in range(8):
        for b in range(2):
            dw_all[b, l * 24 : (l + 1) * 24, :] = dw_in[l // 2, l % 2, b]
    for b in range(2):
        gain[b] = jnp.broadcast_to(dw_all[b, :, 49:50], (192, 128))
    emb_t[...] = pe[:, :, 1].reshape(384, 192).astype(F32).T.astype(BF)
    for k in (1, 2, 3):
        xk = lax.rem(x + k, 4)
        arrived(w_own.at[xk], r_w.at[10 + xk])
    send(w_own, w_other, s_w.at[11], r_w.at[14], device(x, y, h, t, 1 - c))

    own[5].wait()
    for k, flip in [(0, 0)] + others[4:] + others[:4]:
        src = ys[k] * 2 + lax.rem(h + flip, 2)
        if (k, flip) != (0, 0):
            arrived(x_in.at[src], r_x.at[src])
        flat[...] = x_in[src].astype(F32).reshape(640, 128)
        place = pl.ds(pl.multiple_of(src * 48, 16), 48)

        @pl.loop(0, 16)
        def _(r):
            part = flat[pl.ds(r, 40, stride=16), :]
            xt[r, place, :] = jnp.concatenate([part, jnp.zeros((8, 128), F32)], axis=0).astype(BF)

    own[3].wait()

    def sea_rows(r):
        return sea_in[pl.ds(r, 1), :].astype(F32)

    @pl.loop(0, 4)
    def _(n):
        for q in range(2):
            r = 4 * n + 2 * q
            both = jnp.concatenate([xt[r], xt[r + 1]], axis=1)
            stem = jnp.dot(emb_t[...], both, preferred_element_type=F32)
            state[0, r] = (stem[:, :128] * sea_rows(r)).astype(BF)
            state[0, r + 1] = (stem[:, 128:] * sea_rows(r + 1)).astype(BF)

    lane = lax.broadcasted_iota(jnp.int32, (16, 128), 1)

    def group(g):
        return pl.ds(pl.multiple_of(g * 16, 16), 16)

    def rim_copy(b, p):
        return remote(
            state.at[b, pl.ds(13, 3), pl.ds(p * 16, 16), :], fold_in.at[b, col_block],
            s_f1.at[b, p], r_f1.at[b, col_block], device(x, y, p % 2, p // 4, (p // 2) % 2),
        )

    def ghost_copy(b, j):
        tj, cj, sj = j // 4, (j // 2) % 2, j % 2
        return remote(
            fold_out.at[b, j], north.at[b, :, :, group(line), :],
            s_f3.at[b, j], r_f3.at[b, line], device(x, y, sj ^ cj, tj, cj),
        )

    def row_copies(b):
        return (
            remote(state.at[b, pl.ds(13, 3)], south.at[b], s_halo.at[b, 0], r_halo.at[b, 0], north_dev),
            remote(state.at[b, pl.ds(0, 3)], north.at[b, 0], s_halo.at[b, 1], r_halo.at[b, 1], south_dev),
        )

    def side_copies(b):
        return (
            remote(sides.at[b], sides_s.at[b], s_halo.at[b, 4], r_halo.at[b, 4], north_dev),
            remote(sides.at[b], sides_n.at[b], s_halo.at[b, 5], r_halo.at[b, 5], south_dev),
        )

    def start_pair(pair):
        @pl.when(has_north)
        def _():
            pair[0].start()

        @pl.when(has_south)
        def _():
            pair[1].start()

    def halo_start(b):
        @pl.when(on_line)
        def _():
            for p in range(GROUPS):
                @pl.when(line == p)
                def _():
                    fold_in[b, col_block] = state[b, 13:16, p * 16 : (p + 1) * 16, :]

                @pl.when(line != p)
                def _():
                    rim_copy(b, p).start()

        start_pair(row_copies(b))

        @pl.loop(0, GROUPS)
        def _(g):
            ch = group(g)
            to_e = jnp.zeros((16, 128), F32)
            to_w = jnp.zeros((16, 128), F32)
            for r in range(16):
                v = state[b, r, ch, :].astype(F32)
                xrow[r + 3, ch, :] = v
                to_e = jnp.where(
                    (lane >= 3 * r) & (lane < 3 * r + 3), pltpu.roll(v, (3 * r - 125) % 128, 1), to_e
                )
                to_w = jnp.where(
                    (lane >= 64 + 3 * r) & (lane < 67 + 3 * r), pltpu.roll(v, 64 + 3 * r, 1), to_w
                )
            pack_e[b, ch, :] = to_e.astype(BF)
            pack_w[b, ch, :] = to_w.astype(BF)

        send(pack_e.at[b], from_w.at[b], s_halo.at[b, 2], r_halo.at[b, 2], east)
        send(pack_w.at[b], from_e.at[b], s_halo.at[b, 3], r_halo.at[b, 3], west)

    def fold(b):
        for k in range(1, 16):
            j = lax.rem(col_block + k, 16)
            arrived(fold_in.at[b, j], r_f1.at[b, j])
        rim = jnp.concatenate([fold_in[b, j].reshape(48, 128) for j in range(16)], axis=1)

        @pl.loop(0, 8)
        def _(j):
            got = jnp.dot(rim, onehot[j], preferred_element_type=F32).astype(BF)
            for q in range(2):
                for k in range(3):
                    fold_out[b, 2 * j + q, 0, k] = got[(2 - k) * 16 : (3 - k) * 16, q * 128 : (q + 1) * 128]

        @pl.loop(0, 16)
        def _(j):
            for k in range(3):
                after = fold_out[b, lax.rem(j + 1, 16), 0, k].astype(F32)
                before = fold_out[b, lax.rem(j + 15, 16), 0, k].astype(F32)
                fold_out[b, j, 1, k] = jnp.where(lane < 64, after, before).astype(BF)

        for j in range(16):
            @pl.when(col_block == j)
            def _():
                north[b, :, :, group(line), :] = fold_out[b, j]

            @pl.when(col_block != j)
            def _():
                ghost_copy(b, j).start()

    def halo_middle(b):
        @pl.when(on_line & (line < GROUPS))
        def _():
            fold(b)

        arrived(from_w.at[b], r_halo.at[b, 2])
        arrived(from_e.at[b], r_halo.at[b, 3])
        west_lanes = lax.broadcasted_iota(jnp.int32, (192, 128), 1) < 64
        sides[b] = jnp.where(west_lanes, from_w[b].astype(F32), from_e[b].astype(F32)).astype(BF)
        start_pair(side_copies(b))

    def halo_end(b):
        @pl.when(has_south)
        def _():
            arrived(south.at[b], r_halo.at[b, 0])
            arrived(sides_s.at[b], r_halo.at[b, 4])

        @pl.when(jnp.logical_not(has_south))
        def _():
            south[b] = jnp.zeros((3, 192, 128), BF)
            sides_s[b] = jnp.zeros((192, 128), BF)

        @pl.when(has_north)
        def _():
            arrived(north.at[b, 0], r_halo.at[b, 1])
            arrived(sides_n.at[b], r_halo.at[b, 5])

        @pl.when(on_line)
        def _():
            for p in range(GROUPS):
                @pl.when(line != p)
                def _():
                    arrived(north.at[b, :, :, pl.ds(p * 16, 16), :], r_f3.at[b, p])

    def halo_sent(b):
        for pair in (row_copies(b), side_copies(b)):
            @pl.when(has_north)
            def _():
                pair[0].wait_send()

            @pl.when(has_south)
            def _():
                pair[1].wait_send()

        @pl.when(on_line)
        def _():
            for p in range(GROUPS):
                @pl.when(line != p)
                def _():
                    rim_copy(b, p).wait_send()

            @pl.when(line < GROUPS)
            def _():
                for j in range(16):
                    @pl.when(col_block != j)
                    def _():
                        ghost_copy(b, j).wait_send()

    def side_tile(tile, r):
        left = pltpu.roll(tile, (125 - 3 * r) % 128, 1)
        right = pltpu.roll(tile, (64 - 3 * r) % 128, 1)
        return jnp.where(lane < 64, right, left)

    def depthwise(b, inner):
        spans = ((3, 13),) if inner else ((0, 3), (13, 16))

        @pl.loop(0, GROUPS)
        def _(g):
            ch = group(g)
            if inner:
                tile = sides[b, ch, :].astype(F32)
                for r in range(16):
                    srow[r + 3, ch, :] = side_tile(tile, r)
            else:
                tile = sides_s[b, ch, :].astype(F32)
                for r in range(3):
                    xrow[r, ch, :] = south[b, r, ch, :].astype(F32)
                    srow[r, ch, :] = side_tile(tile, r + 13)
                    xrow[r + 19, ch, :] = north[b, 0, r, ch, :].astype(F32)

                @pl.when(has_north)
                def _():
                    tile = sides_n[b, ch, :].astype(F32)
                    for r in range(3):
                        srow[r + 19, ch, :] = side_tile(tile, r)

                @pl.when(on_line)
                def _():
                    for r in range(3):
                        srow[r + 19, ch, :] = north[b, 1, r, ch, :].astype(F32)

            taps = dw_all[b, ch, :]
            acc = [None] * 16
            for e in range(7):
                w = [jnp.broadcast_to(taps[:, a * 7 + e : a * 7 + e + 1], (16, 128)) for a in range(7)]
                o = e - 3
                for lo, hi in spans:
                    for r in range(lo, hi + 6):
                        v = xrow[r, ch, :]
                        if o < 0:
                            v = pltpu.roll(jnp.where(lane >= 128 + o, srow[r, ch, :], v), -o, 1)
                        elif o > 0:
                            v = pltpu.roll(jnp.where(lane < o, srow[r, ch, :], v), 128 - o, 1)
                        for a in range(7):
                            q = r - a
                            if lo <= q < hi:
                                term = w[a] * v
                                acc[q] = term if acc[q] is None else acc[q] + term
            for lo, hi in spans:
                for q in range(lo, hi):
                    conv[q, ch, :] = acc[q]

    def pointwise(b, first):
        @pl.loop(0, 2)
        def _(n):
            for q in range(2):
                i = first(n) + q
                parts = []
                for k in range(2):
                    cv = conv[2 * i + k]
                    mu = jnp.sum(cv, axis=0, keepdims=True) * (1.0 / 192)
                    var = jnp.sum(cv * cv, axis=0, keepdims=True) * (1.0 / 192) - mu * mu
                    parts.append(((cv - mu) * lax.rsqrt(var + 1e-6) * gain[b]).astype(BF))
                normed = jnp.concatenate(parts, axis=1)
                branch = jnp.zeros((192, 256), F32)
                for side, w in enumerate((w_own, w_other)):
                    pre = jnp.dot(w[2 * b].reshape(384, 192), normed, preferred_element_type=F32)
                    hidden = jax.nn.gelu(pre, approximate=True).astype(BF)
                    branch = branch + jnp.dot(down_t[b, side], hidden, preferred_element_type=F32)
                for k in range(2):
                    r = 2 * i + k
                    new = (state[b, r].astype(F32) + branch[:, k * 128 : (k + 1) * 128]) * sea_rows(r)
                    if b == 0:
                        state[1, r] = new.astype(BF)
                    else:
                        out_f[pl.ds(r, 192, stride=16), :] = new

    for b in range(2):
        halo_start(b)
        if b == 0:
            arrived(w_other, r_w.at[14])
            for bb in range(2):
                for side, w in enumerate((w_own, w_other)):
                    down_t[bb, side] = w[2 * bb + 1].reshape(384, 192).astype(F32).T.astype(BF)
        halo_middle(b)
        depthwise(b, True)
        pointwise(b, lambda n: 2 + 2 * n)
        halo_end(b)
        depthwise(b, False)
        pointwise(b, lambda n: 6 * n)

    def chunk(l):
        chans = pl.ds(l * 24, 24)
        out_b[chans] = out_f[pl.ds(pl.multiple_of(l * 384, 384), 384), :].reshape(24, 16, 128).astype(BF)
        return out_b.at[chans]

    for i, (k, flip) in enumerate(others):
        hh = lax.rem(h + flip, 2)
        send(
            chunk(ys[k] * 2 + hh), out.at[:, my_rows, my_cols], s_o.at[i], r_o.at[lev], device(x, ys[k], hh, t, c)
        )
    last = pltpu.make_async_copy(chunk(lev), out.at[:, my_rows, my_cols], s_o.at[7])
    last.start()
    for k, flip in others:
        hh = lax.rem(h + flip, 2)
        rows, cols = cells_of(ys[k], hh)
        arrived(out.at[:, rows, cols], r_o.at[ys[k] * 2 + hh])
    last.wait()
    for cp in sends:
        cp.wait_send()
    for b in range(2):
        halo_sent(b)


def body(fields, sea_mask, fold_partner, embed_weight, dw_weight, ln_gain, up_weight, down_weight):
    partner = fold_partner.reshape(16, 128)
    hbm = pl.BlockSpec(memory_space=pl.ANY)
    dma = pltpu.SemaphoreType.DMA
    scratch = [
        pltpu.VMEM((8, 40, 16, 128), BF),
        pltpu.VMEM((16, 128), jnp.int32),
        pltpu.VMEM((16, 128), jnp.int32),
        pltpu.VMEM((40, 192), BF),
        pltpu.VMEM((2, 24, 7, 7), F32),
        pltpu.VMEM((2, 24), BF),
        pltpu.VMEM((16, 384, 128), BF),
        pltpu.VMEM((640, 128), F32),
        pltpu.VMEM((4, 2, 2, 48, 192), BF),
        pltpu.VMEM((4, 2, 2, 24, 128), F32),
        pltpu.VMEM((2, 192, 128), F32),
        pltpu.VMEM((192, 384), BF),
        pltpu.VMEM((4, 4, 2, 48, 192), BF),
        pltpu.VMEM((4, 4, 2, 48, 192), BF),
        pltpu.VMEM((2, 2, 192, 384), BF),
        pltpu.VMEM((2, 192, 128), F32),
        pltpu.VMEM((16, 192, 128), F32),
        pltpu.VMEM((2, 16, 192, 128), BF),
        pltpu.VMEM((2, 3, 192, 128), BF),
        pltpu.VMEM((2, 2, 3, 192, 128), BF),
        pltpu.VMEM((2, 192, 128), BF),
        pltpu.VMEM((2, 192, 128), BF),
        pltpu.VMEM((2, 192, 128), BF),
        pltpu.VMEM((2, 192, 128), BF),
        pltpu.VMEM((2, 192, 128), BF),
        pltpu.VMEM((2, 192, 128), BF),
        pltpu.VMEM((2, 192, 128), BF),
        pltpu.VMEM((22, 192, 128), F32),
        pltpu.VMEM((22, 192, 128), F32),
        pltpu.VMEM((8, 2048, 256), BF),
        pltpu.VMEM((2, 16, 3, 16, 128), BF),
        pltpu.VMEM((2, 16, 2, 3, 16, 128), BF),
        pltpu.VMEM((192 * 16, 128), F32),
        pltpu.VMEM((192, 16, 128), BF),
        dma((7,)), dma((8,)),
        dma((7,)),
        dma((12,)), dma((15,)),
        dma((2, 6)), dma((2, 6)),
        dma((2, 12)), dma((2, 16)),
        dma((2, 16)), dma((2, 12)),
        dma((8,)), dma((8,)),
    ]
    return pl.pallas_call(
        kernel,
        out_shape=jax.ShapeDtypeStruct((24, 64, 256), BF),
        in_specs=[hbm] * 8,
        out_specs=hbm,
        scratch_shapes=scratch,
        compiler_params=pltpu.CompilerParams(
            collective_id=0, has_side_effects=True, vmem_limit_bytes=60 * 1024 * 1024
        ),
    )(fields, sea_mask, partner, embed_weight, dw_weight, ln_gain, up_weight, down_weight)


def solution(mesh):
    in_specs = (
        P("lev", "gy", "gx"),
        P("gy", "gx"),
        P(),
        P("lev", None),
        P(None, "lev", None, None),
        P(None, "lev"),
        P(None, "lev", None),
        P(None, "lev", None),
    )
    out_specs = P("lev", "gy", "gx")
    return jax.shard_map(body, mesh=mesh, in_specs=in_specs, out_specs=out_specs, check_vma=False)
```

time: 1110 us -> 127 us (0.11)
  waiting for transfers between devices: 929 us -> 0 us
  Pallas kernels: 0 us -> 123 us
  local copies, waits for them, and re-layouts: 46.6 us -> 3.72 us
  other arithmetic: 41.6 us -> 0 us
  blocking collectives: 36.3 us -> 0 us
  matrix products: 19.6 us -> 0 us
  between operations: 14.5 us -> 0.01 us
  starting transfers between devices: 13.1 us -> 0 us
    reduce_scatter x3 -> x0, waiting for transfers between devices: 448 us -> none  [the longest x2 304 us: body(): lax.psum_scatter(rounded(part).astype(jnp.bfloat16), 'lev', scatter_dimen...]
    all_gather x2 -> x0, waiting for transfers between devices: 268 us -> none  [body(): lax.all_gather(normed.reshape(chan_local, cells), 'lev', axis=0, tiled=True)]
    psum x2 -> x0, waiting for transfers between devices: 193 us -> none  [body(): lax.psum(jnp.sum(conv * conv, axis=0).astype(jnp.bfloat16), 'lev')]
    pallas_call x0 -> x1, Pallas kernels: none -> 123 us  [body(): pl.pallas_call(kernel, out_shape=jax.ShapeDtypeStruct((24, 64, 256), BF),...]
    all_gather x2 -> x0, blocking collectives: 36.3 us -> none  [body(): whole_rim = lax.all_gather(rim, 'gx', axis=2, tiled=True)]
    reduce_sum x2 -> x0, other arithmetic: 28.9 us -> none  [body(): jnp.sum(conv, axis=0).astype(jnp.bfloat16)]
    rev x2 -> x0, local copies, waits for them, and re-layouts: 21 us -> none  [body(): fold_rows = jnp.take(whole_rim[:, ::-1, :], fold_cols, axis=2)]
    dot_general x3 -> x0, matrix products: 19.6 us -> none  [the longest x2 15.1 us: body(): lax.dot_general(down_local, hidden, (((0,), (0,)), ((), ())), preferred_e...]
  transfers between devices with their start and end apart: 15 -> 0, of which waited for: 11 -> 0; matrix products, arithmetic and copies ran while one was open for 3% -> 0% of each run, Pallas kernels for 0% -> 0%
where the time goes in v2:
time: 127 us
  Pallas kernels  123 us (97%)
  local copies, waits for them, and re-layouts  3.72 us (3%)
    pallas_call x1, Pallas kernels, body(): pl.pallas_call(kernel, out_shape=jax.ShapeDtypeStruct((24, 64, 256), BF),...  123 us
    unnamed x2, local copies, waits for them, and re-layouts  3.72 us

profile of v2, /device:TPU:127, one launch (start us, length us, event | category | flops | bytes accessed | tf_op | source)
XLA Modules:
  0.0 126.7 jit_solution(18062934816538074220)
XLA Ops:
  0.0 1.6 %copy.9.dw_weight = f32[2,24,7,7]{3,2,1,0:T(8,128)} copy(f32[2,24,7,7]{1,0,3,2:T(2,128)} %param.12) | data formatting | bytes 18816 | tf_op args[4]
  1.6 122.9 %shard_map.82 = bf16[24,64,256]{2,1,0:T(8,128)(2,1)} custom-call(bf16[40,64,256]{2,1,0:T(8,128)(2,1)} %fields.1, s32[64,256]{1,0:T(8,128)} %sea.1, s32[16,128]{1,0:T(8,128)} %bitcast.1, bf16[40,192]{1,0:T(8,128)(2,1)} %embed.1, f32[2,24,7,7]{3,2,1,0:T(8,128)} %copy.9.dw_weight, bf16[2,24]{1,0:T(2,128)(2,1)} %ln_gain.1, bf16[2,96,192]{2,1,0:T(8,128)(2,1)} %up.1, ...), custom_call_target="tpu_custom_call" | custom-call | tf_op jit(solution)/shard_map/pallas_call | solution.py:548
  124.6 2.1 %copy.11 = bf16[24,64,256]{2,1,0:T(8,128)(2,1)} copy(bf16[24,64,256]{2,1,0:T(8,128)(2,1)} %shard_map.82) | data formatting | bytes 1572864

commit v3 on v2

--- a/solution.py
+++ b/solution.py
@@ -11,12 +11,17 @@
 GROUPS = 12
 
 
+def twice_gelu(v):
+    inner = v * (0.7978845608028654 + 0.035677408136300125 * (v * v))
+    return v + v * jnp.tanh(inner)
+
+
 def kernel(
     fields, sea, partner, embed, dw_weight, ln_gain, up, down,
     out,
     x_in, sea_in, partner_in, embed_in, dw_raw, gain_raw,
-    xt, flat, pe, dw_in, dw_all, emb_t, w_own, w_other, down_t, gain, conv,
-    state, south, north, sides, sides_s, sides_n, pack_e, pack_w, from_w, from_e, xrow, srow,
+    xt, flat, pe, dw_in, dw_all, taps, end_taps, emb_t, w_own, w_other, down_t, gain, conv,
+    state, south, north, diff, diff_s, diff_n, pack, from_w, from_e, xrow,
     onehot, fold_in, fold_out, out_f, out_b,
     s_x, r_x, s_loc, s_w, r_w, s_halo, r_halo, s_f1, r_f1, s_f3, r_f3, s_o, r_o,
 ):
@@ -189,6 +194,19 @@
             dw_all[b, l * 24 : (l + 1) * 24, :] = dw_in[l // 2, l % 2, b]
     for b in range(2):
         gain[b] = jnp.broadcast_to(dw_all[b, :, 49:50], (192, 128))
+    west16 = lax.rem(lax.broadcasted_iota(jnp.int32, (16, 128), 1), 6) >= 3
+    for b in range(2):
+        @pl.loop(0, GROUPS)
+        def _(g):
+            ch = pl.ds(pl.multiple_of(g * 16, 16), 16)
+            row = dw_all[b, ch, :]
+            wide = [jnp.broadcast_to(row[:, k : k + 1], (16, 128)) for k in range(49)]
+            for k in range(49):
+                taps[b, k, ch, :] = wide[k]
+            for a in range(7):
+                for d in range(3):
+                    end_taps[b, a * 3 + d, ch, :] = jnp.where(west16, wide[a * 7 + d], wide[a * 7 + 4 + d])
+
     emb_t[...] = pe[:, :, 1].reshape(384, 192).astype(F32).T.astype(BF)
     for k in (1, 2, 3):
         xk = lax.rem(x + k, 4)
@@ -224,6 +242,11 @@
 
     lane = lax.broadcasted_iota(jnp.int32, (16, 128), 1)
 
+    wide_lane = lax.broadcasted_iota(jnp.int32, (192, 128), 1)
+    west_slot = lax.rem(wide_lane, 6) >= 3
+    place = lax.rem(wide_lane, 3)
+    row_ends = (wide_lane < 3) | (wide_lane >= 125)
+
     def group(g):
         return pl.ds(pl.multiple_of(g * 16, 16), 16)
 
@@ -248,8 +271,8 @@
 
     def side_copies(b):
         return (
-            remote(sides.at[b], sides_s.at[b], s_halo.at[b, 4], r_halo.at[b, 4], north_dev),
-            remote(sides.at[b], sides_n.at[b], s_halo.at[b, 5], r_halo.at[b, 5], south_dev),
+            remote(diff.at[b], diff_s.at[b], s_halo.at[b, 4], r_halo.at[b, 4], north_dev),
+            remote(diff.at[b], diff_n.at[b], s_halo.at[b, 5], r_halo.at[b, 5], south_dev),
         )
 
     def start_pair(pair):
@@ -275,25 +298,19 @@
 
         start_pair(row_copies(b))
 
-        @pl.loop(0, GROUPS)
+        @pl.loop(0, 2)
         def _(g):
-            ch = group(g)
-            to_e = jnp.zeros((16, 128), F32)
-            to_w = jnp.zeros((16, 128), F32)
+            ch = pl.ds(pl.multiple_of(g * 96, 96), 96)
+            lane96 = lax.broadcasted_iota(jnp.int32, (96, 128), 1)
+            tile = jnp.zeros((96, 128), F32)
             for r in range(16):
                 v = state[b, r, ch, :].astype(F32)
                 xrow[r + 3, ch, :] = v
-                to_e = jnp.where(
-                    (lane >= 3 * r) & (lane < 3 * r + 3), pltpu.roll(v, (3 * r - 125) % 128, 1), to_e
-                )
-                to_w = jnp.where(
-                    (lane >= 64 + 3 * r) & (lane < 67 + 3 * r), pltpu.roll(v, 64 + 3 * r, 1), to_w
-                )
-            pack_e[b, ch, :] = to_e.astype(BF)
-            pack_w[b, ch, :] = to_w.astype(BF)
-
-        send(pack_e.at[b], from_w.at[b], s_halo.at[b, 2], r_halo.at[b, 2], east)
-        send(pack_w.at[b], from_e.at[b], s_halo.at[b, 3], r_halo.at[b, 3], west)
+                tile = jnp.where((lane96 >= 6 * r) & (lane96 < 6 * r + 6), pltpu.roll(v, 6 * r + 3, 1), tile)
+            pack[b, ch, :] = tile.astype(BF)
+
+        send(pack.at[b], from_w.at[b], s_halo.at[b, 2], r_halo.at[b, 2], east)
+        send(pack.at[b], from_e.at[b], s_halo.at[b, 3], r_halo.at[b, 3], west)
 
     def fold(b):
         for k in range(1, 16):
@@ -331,25 +348,29 @@
 
         arrived(from_w.at[b], r_halo.at[b, 2])
         arrived(from_e.at[b], r_halo.at[b, 3])
-        west_lanes = lax.broadcasted_iota(jnp.int32, (192, 128), 1) < 64
-        sides[b] = jnp.where(west_lanes, from_w[b].astype(F32), from_e[b].astype(F32)).astype(BF)
+        mine = pack[b].astype(F32)
+        diff[b] = jnp.where(
+            west_slot,
+            pltpu.roll(from_w[b].astype(F32) - mine, 3, 1),
+            pltpu.roll(from_e[b].astype(F32) - mine, 125, 1),
+        )
         start_pair(side_copies(b))
 
     def halo_end(b):
         @pl.when(has_south)
         def _():
             arrived(south.at[b], r_halo.at[b, 0])
-            arrived(sides_s.at[b], r_halo.at[b, 4])
+            arrived(diff_s.at[b], r_halo.at[b, 4])
 
         @pl.when(jnp.logical_not(has_south))
         def _():
             south[b] = jnp.zeros((3, 192, 128), BF)
-            sides_s[b] = jnp.zeros((192, 128), BF)
+            diff_s[b] = jnp.zeros((192, 128), F32)
 
         @pl.when(has_north)
         def _():
             arrived(north.at[b, 0], r_halo.at[b, 1])
-            arrived(sides_n.at[b], r_halo.at[b, 5])
+            arrived(diff_n.at[b], r_halo.at[b, 5])
 
         @pl.when(on_line)
         def _():
@@ -357,6 +378,18 @@
                 @pl.when(line != p)
                 def _():
                     arrived(north.at[b, :, :, pl.ds(p * 16, 16), :], r_f3.at[b, p])
+
+            @pl.loop(0, GROUPS)
+            def _(g):
+                ch = group(g)
+                tile = jnp.zeros((16, 128), F32)
+                for r in range(3):
+                    d = north[b, 1, r, ch, :].astype(F32) - north[b, 0, r, ch, :].astype(F32)
+                    tile = jnp.where((lane >= 6 * r) & (lane < 6 * r + 3), pltpu.roll(d, 6 * r, 1), tile)
+                    tile = jnp.where(
+                        (lane >= 6 * r + 3) & (lane < 6 * r + 6), pltpu.roll(d, 6 * r + 6, 1), tile
+                    )
+                diff_n[b, ch, :] = tile
 
     def halo_sent(b):
         for pair in (row_copies(b), side_copies(b)):
@@ -382,59 +415,58 @@
                     def _():
                         ghost_copy(b, j).wait_send()
 
-    def side_tile(tile, r):
-        left = pltpu.roll(tile, (125 - 3 * r) % 128, 1)
-        right = pltpu.roll(tile, (64 - 3 * r) % 128, 1)
-        return jnp.where(lane < 64, right, left)
-
     def depthwise(b, inner):
         spans = ((3, 13),) if inner else ((0, 3), (13, 16))
 
         @pl.loop(0, GROUPS)
         def _(g):
             ch = group(g)
-            if inner:
-                tile = sides[b, ch, :].astype(F32)
-                for r in range(16):
-                    srow[r + 3, ch, :] = side_tile(tile, r)
-            else:
-                tile = sides_s[b, ch, :].astype(F32)
+            if not inner:
                 for r in range(3):
                     xrow[r, ch, :] = south[b, r, ch, :].astype(F32)
-                    srow[r, ch, :] = side_tile(tile, r + 13)
                     xrow[r + 19, ch, :] = north[b, 0, r, ch, :].astype(F32)
-
-                @pl.when(has_north)
-                def _():
-                    tile = sides_n[b, ch, :].astype(F32)
-                    for r in range(3):
-                        srow[r + 19, ch, :] = side_tile(tile, r)
-
-                @pl.when(on_line)
-                def _():
-                    for r in range(3):
-                        srow[r + 19, ch, :] = north[b, 1, r, ch, :].astype(F32)
-
-            taps = dw_all[b, ch, :]
-            acc = [None] * 16
+            xs = {r: xrow[r, ch, :] for lo, hi in spans for r in range(lo, hi + 6)}
+            acc = {}
             for e in range(7):
-                w = [jnp.broadcast_to(taps[:, a * 7 + e : a * 7 + e + 1], (16, 128)) for a in range(7)]
-                o = e - 3
+                w = [taps[b, a * 7 + e, ch, :] for a in range(7)]
                 for lo, hi in spans:
-                    for r in range(lo, hi + 6):
-                        v = xrow[r, ch, :]
-                        if o < 0:
-                            v = pltpu.roll(jnp.where(lane >= 128 + o, srow[r, ch, :], v), -o, 1)
-                        elif o > 0:
-                            v = pltpu.roll(jnp.where(lane < o, srow[r, ch, :], v), 128 - o, 1)
-                        for a in range(7):
-                            q = r - a
-                            if lo <= q < hi:
-                                term = w[a] * v
-                                acc[q] = term if acc[q] is None else acc[q] + term
-            for lo, hi in spans:
-                for q in range(lo, hi):
-                    conv[q, ch, :] = acc[q]
+                    for q in range(lo, hi):
+                        v = w[0] * xs[q]
+                        for a in range(1, 7):
+                            v = v + w[a] * xs[q + a]
+                        if e != 3:
+                            v = pltpu.roll(v, (3 - e) % 128, 1)
+                        acc[q] = v if e == 0 else acc[q] + v
+            for q in acc:
+                conv[q, ch, :] = acc[q]
+
+    def correct(b, inner):
+        tile = diff[b]
+        rows = [(q, q - 3) for q in range(3, 13)]
+        if not inner:
+            tile = jnp.where(
+                wide_lane < 18,
+                pltpu.roll(diff_s[b], 50, 1),
+                jnp.where(
+                    wide_lane < 54,
+                    pltpu.roll(tile, 18, 1),
+                    jnp.where(wide_lane < 90, pltpu.roll(tile, 122, 1), pltpu.roll(diff_n[b], 90, 1)),
+                ),
+            )
+            rows = [(0, 0), (1, 1), (2, 2), (13, 9), (14, 10), (15, 11)]
+        sums = [None] * 3
+        for a in range(7):
+            moved = pltpu.roll(tile, (-6 * a) % 128, 1) if a else tile
+            for d in range(3):
+                term = end_taps[b, a * 3 + d] * moved
+                sums[d] = term if a == 0 else sums[d] + term
+        fix = jnp.where(west_slot, sums[0], sums[2])
+        fix = fix + jnp.where(west_slot & (place <= 1), pltpu.roll(sums[1], 127, 1), 0.0)
+        fix = fix + jnp.where(~west_slot & (place >= 1), pltpu.roll(sums[1], 1, 1), 0.0)
+        fix = fix + jnp.where(west_slot & (place == 0), pltpu.roll(sums[2], 126, 1), 0.0)
+        fix = fix + jnp.where(~west_slot & (place == 2), pltpu.roll(sums[0], 2, 1), 0.0)
+        for q, k in rows:
+            conv[q] += jnp.where(row_ends, pltpu.roll(fix, (-6 * k - 3) % 128, 1), 0.0)
 
     def pointwise(b, first):
         @pl.loop(0, 2)
@@ -451,11 +483,11 @@
                 branch = jnp.zeros((192, 256), F32)
                 for side, w in enumerate((w_own, w_other)):
                     pre = jnp.dot(w[2 * b].reshape(384, 192), normed, preferred_element_type=F32)
-                    hidden = jax.nn.gelu(pre, approximate=True).astype(BF)
+                    hidden = twice_gelu(pre).astype(BF)
                     branch = branch + jnp.dot(down_t[b, side], hidden, preferred_element_type=F32)
                 for k in range(2):
                     r = 2 * i + k
-                    new = (state[b, r].astype(F32) + branch[:, k * 128 : (k + 1) * 128]) * sea_rows(r)
+                    new = (state[b, r].astype(F32) + 0.5 * branch[:, k * 128 : (k + 1) * 128]) * sea_rows(r)
                     if b == 0:
                         state[1, r] = new.astype(BF)
                     else:
@@ -463,16 +495,18 @@
 
     for b in range(2):
         halo_start(b)
+        depthwise(b, True)
         if b == 0:
             arrived(w_other, r_w.at[14])
             for bb in range(2):
                 for side, w in enumerate((w_own, w_other)):
                     down_t[bb, side] = w[2 * bb + 1].reshape(384, 192).astype(F32).T.astype(BF)
         halo_middle(b)
-        depthwise(b, True)
+        correct(b, True)
         pointwise(b, lambda n: 2 + 2 * n)
         halo_end(b)
         depthwise(b, False)
+        correct(b, False)
         pointwise(b, lambda n: 6 * n)
 
     def chunk(l):
@@ -514,6 +548,8 @@
         pltpu.VMEM((4, 2, 2, 48, 192), BF),
         pltpu.VMEM((4, 2, 2, 24, 128), F32),
         pltpu.VMEM((2, 192, 128), F32),
+        pltpu.VMEM((2, 49, 192, 128), F32),
+        pltpu.VMEM((2, 21, 192, 128), F32),
         pltpu.VMEM((192, 384), BF),
         pltpu.VMEM((4, 4, 2, 48, 192), BF),
         pltpu.VMEM((4, 4, 2, 48, 192), BF),
@@ -523,14 +559,12 @@
         pltpu.VMEM((2, 16, 192, 128), BF),
         pltpu.VMEM((2, 3, 192, 128), BF),
         pltpu.VMEM((2, 2, 3, 192, 128), BF),
+        pltpu.VMEM((2, 192, 128), F32),
+        pltpu.VMEM((2, 192, 128), F32),
+        pltpu.VMEM((2, 192, 128), F32),
         pltpu.VMEM((2, 192, 128), BF),
         pltpu.VMEM((2, 192, 128), BF),
         pltpu.VMEM((2, 192, 128), BF),
-        pltpu.VMEM((2, 192, 128), BF),
-        pltpu.VMEM((2, 192, 128), BF),
-        pltpu.VMEM((2, 192, 128), BF),
-        pltpu.VMEM((2, 192, 128), BF),
-        pltpu.VMEM((22, 192, 128), F32),
         pltpu.VMEM((22, 192, 128), F32),
         pltpu.VMEM((8, 2048, 256), BF),
         pltpu.VMEM((2, 16, 3, 16, 128), BF),

time: 127 us -> 121 us (0.953)
  Pallas kernels: 123 us -> 117 us
    pallas_call x1, Pallas kernels: 123 us -> 117 us  [body(): pl.pallas_call(kernel, out_shape=jax.ShapeDtypeStruct((24, 64, 256), BF),...]
where the time goes in v3:
time: 121 us
  Pallas kernels  117 us (97%)
  local copies, waits for them, and re-layouts  3.72 us (3%)
    pallas_call x1, Pallas kernels, body(): pl.pallas_call(kernel, out_shape=jax.ShapeDtypeStruct((24, 64, 256), BF),...  117 us
    unnamed x2, local copies, waits for them, and re-layouts  3.72 us

profile of v3, /device:TPU:127, one launch (start us, length us, event | category | flops | bytes accessed | tf_op | source)
XLA Modules:
  0.0 121.2 jit_solution(11537679588359936602)
XLA Ops:
  0.0 1.6 %copy.9.dw_weight = f32[2,24,7,7]{3,2,1,0:T(8,128)} copy(f32[2,24,7,7]{1,0,3,2:T(2,128)} %param.12) | data formatting | bytes 18816 | tf_op args[4]
  1.6 117.5 %shard_map.82 = bf16[24,64,256]{2,1,0:T(8,128)(2,1)} custom-call(bf16[40,64,256]{2,1,0:T(8,128)(2,1)} %fields.1, s32[64,256]{1,0:T(8,128)} %sea.1, s32[16,128]{1,0:T(8,128)} %bitcast.1, bf16[40,192]{1,0:T(8,128)(2,1)} %embed.1, f32[2,24,7,7]{3,2,1,0:T(8,128)} %copy.9.dw_weight, bf16[2,24]{1,0:T(2,128)(2,1)} %ln_gain.1, bf16[2,96,192]{2,1,0:T(8,128)(2,1)} %up.1, ...), custom_call_target="tpu_custom_call" | custom-call | tf_op jit(solution)/shard_map/pallas_call | solution.py:582
  119.1 2.1 %copy.11 = bf16[24,64,256]{2,1,0:T(8,128)(2,1)} copy(bf16[24,64,256]{2,1,0:T(8,128)(2,1)} %shard_map.82) | data formatting | bytes 1572864

commit v4 on v3

--- a/solution.py
+++ b/solution.py
@@ -22,7 +22,7 @@
     x_in, sea_in, partner_in, embed_in, dw_raw, gain_raw,
     xt, flat, pe, dw_in, dw_all, taps, end_taps, emb_t, w_own, w_other, down_t, gain, conv,
     state, south, north, diff, diff_s, diff_n, pack, from_w, from_e, xrow,
-    onehot, fold_in, fold_out, out_f, out_b,
+    fold_in, fold_out, fold_src, out_f, out_b,
     s_x, r_x, s_loc, s_w, r_w, s_halo, r_halo, s_f1, r_f1, s_f3, r_f3, s_o, r_o,
 ):
     lev = lax.axis_index("lev")
@@ -47,6 +47,7 @@
     col_block = (t * 2 + c) * 2 + s
     line = gx * 2 + h
     on_line = (x == 3) & (rb == 3)
+    permutes = (x == 3) & (rb != 3) & (line < GROUPS)
     has_south = jnp.logical_not((x == 0) & (rb == 0))
     has_north = jnp.logical_not(on_line)
 
@@ -106,23 +107,41 @@
     peers += [device(lax.rem(x + k, 4), y, h, t, c) for k in (1, 2, 3)]
     peers += [device(x, y, h, t, 1 - c)]
 
+    def by_line(yy, p):
+        return device(x, yy, lax.rem(p, 2), p // 4, lax.rem(p // 2, 2))
+
+    def permuter(k, p):
+        return by_line(1 + k, p)
+
+    def rim_device(p):
+        return by_line(0, p)
+
     def greet(dev):
         pl.semaphore_signal(barrier, inc=1, device_id=dev, device_id_type=MESH)
 
     for dev in peers:
         greet(dev)
 
+    @pl.when(h == 0)
+    def _():
+        greet(near)
+
     @pl.when(on_line)
     def _():
-        for k in (1, 2, 3):
-            for hh in range(2):
-                for cc in range(2):
-                    greet(device(x, y, hh, lax.rem(t + k, 4), cc))
-        greet(device(x, y, 1 - h, t, 1 - c))
-
-    @pl.when(has_north & (h == 0))
+        @pl.loop(0, GROUPS)
+        def _(p):
+            @pl.when(p // 2 != gx)
+            def _():
+                for k in range(3):
+                    greet(permuter(k, p))
+
+    @pl.when(permutes)
     def _():
-        greet(near)
+        @pl.loop(0, 16)
+        def _(p):
+            @pl.when(p // 2 != gx)
+            def _():
+                greet(rim_device(p))
 
     own[0].wait()
     own[1].wait()
@@ -138,7 +157,8 @@
         )
     pltpu.make_async_copy(up.at[0].at[half_rows, :], slot.at[0], s_loc.at[0]).wait()
 
-    pl.semaphore_wait(barrier, len(peers) + jnp.where(on_line, 13, 1 - h))
+    across = jnp.where(on_line, jnp.where(gx < 6, 30, 36), jnp.where(permutes, 14, 0))
+    pl.semaphore_wait(barrier, len(peers) + 1 - h + across)
 
     sends = []
 
@@ -166,19 +186,6 @@
         send(dw_in.at[y], dw_in.at[y], s_w.at[2 * k + 1], r_w.at[6 + y], dev)
 
     own[4].wait()
-
-    @pl.when(on_line & (line < GROUPS))
-    def _():
-        @pl.loop(0, 8)
-        def _(j):
-            @pl.loop(0, 16)
-            def _(m):
-                source = lax.broadcasted_iota(jnp.int32, (128, 128), 0) + m * 128
-                for q in range(2):
-                    hit = source == partner_in[pl.ds(2 * j + q, 1), :]
-                    onehot[j, pl.ds(pl.multiple_of(m * 128, 128), 128), q * 128 : (q + 1) * 128] = jnp.where(
-                        hit, 1.0, 0.0
-                    ).astype(BF)
 
     for k in (1, 2, 3):
         arrived(pe.at[ys[k]], r_w.at[2 + ys[k]])
@@ -250,17 +257,16 @@
     def group(g):
         return pl.ds(pl.multiple_of(g * 16, 16), 16)
 
-    def rim_copy(b, p):
+    def rim_copy(b, k, p):
         return remote(
-            state.at[b, pl.ds(13, 3), pl.ds(p * 16, 16), :], fold_in.at[b, col_block],
-            s_f1.at[b, p], r_f1.at[b, col_block], device(x, y, p % 2, p // 4, (p // 2) % 2),
+            state.at[b, 15 - k, group(p), :], fold_in.at[b, col_block], s_f1.at[b], r_f1.at[b], permuter(k, p)
         )
 
     def ghost_copy(b, j):
-        tj, cj, sj = j // 4, (j // 2) % 2, j % 2
+        tj, cj, sj = j // 4, lax.rem(j // 2, 2), lax.rem(j, 2)
         return remote(
-            fold_out.at[b, j], north.at[b, :, :, group(line), :],
-            s_f3.at[b, j], r_f3.at[b, line], device(x, y, sj ^ cj, tj, cj),
+            fold_out.at[b, j], north.at[b, :, y - 1, group(line), :],
+            s_f3.at[b], r_f3.at[b], device(x, 0, lax.rem(sj + cj, 2), tj, cj),
         )
 
     def row_copies(b):
@@ -287,14 +293,10 @@
     def halo_start(b):
         @pl.when(on_line)
         def _():
-            for p in range(GROUPS):
-                @pl.when(line == p)
-                def _():
-                    fold_in[b, col_block] = state[b, 13:16, p * 16 : (p + 1) * 16, :]
-
-                @pl.when(line != p)
-                def _():
-                    rim_copy(b, p).start()
+            @pl.loop(0, GROUPS)
+            def _(p):
+                for k in range(3):
+                    rim_copy(b, k, p).start()
 
         start_pair(row_copies(b))
 
@@ -313,39 +315,28 @@
         send(pack.at[b], from_e.at[b], s_halo.at[b, 3], r_halo.at[b, 3], west)
 
     def fold(b):
-        for k in range(1, 16):
-            j = lax.rem(col_block + k, 16)
-            arrived(fold_in.at[b, j], r_f1.at[b, j])
-        rim = jnp.concatenate([fold_in[b, j].reshape(48, 128) for j in range(16)], axis=1)
-
-        @pl.loop(0, 8)
-        def _(j):
-            got = jnp.dot(rim, onehot[j], preferred_element_type=F32).astype(BF)
-            for q in range(2):
-                for k in range(3):
-                    fold_out[b, 2 * j + q, 0, k] = got[(2 - k) * 16 : (3 - k) * 16, q * 128 : (q + 1) * 128]
+        arrived(fold_in.at[b], r_f1.at[b])
+        for j in range(16):
+            fold_src[j] = fold_in[b, j].astype(F32)
+
+        ghosts = []
+        for j in range(16):
+            column = jnp.broadcast_to(partner_in[j : j + 1, :], (16, 128))
+            within, block = column & 127, column >> 7
+            picked = [jnp.take_along_axis(fold_src[i], within, axis=1) for i in range(16)]
+            for bit in range(4):
+                odd = ((block >> bit) & 1) == 1
+                picked = [jnp.where(odd, picked[i + 1], picked[i]) for i in range(0, len(picked), 2)]
+            ghosts.append(picked[0])
+        for j in range(16):
+            fold_out[b, j, 0] = ghosts[j].astype(BF)
+            fold_out[b, j, 1] = jnp.where(lane < 64, ghosts[(j + 1) % 16], ghosts[j - 1]).astype(BF)
 
         @pl.loop(0, 16)
         def _(j):
-            for k in range(3):
-                after = fold_out[b, lax.rem(j + 1, 16), 0, k].astype(F32)
-                before = fold_out[b, lax.rem(j + 15, 16), 0, k].astype(F32)
-                fold_out[b, j, 1, k] = jnp.where(lane < 64, after, before).astype(BF)
-
-        for j in range(16):
-            @pl.when(col_block == j)
-            def _():
-                north[b, :, :, group(line), :] = fold_out[b, j]
-
-            @pl.when(col_block != j)
-            def _():
-                ghost_copy(b, j).start()
+            ghost_copy(b, j).start()
 
     def halo_middle(b):
-        @pl.when(on_line & (line < GROUPS))
-        def _():
-            fold(b)
-
         arrived(from_w.at[b], r_halo.at[b, 2])
         arrived(from_e.at[b], r_halo.at[b, 3])
         mine = pack[b].astype(F32)
@@ -356,7 +347,11 @@
         )
         start_pair(side_copies(b))
 
-    def halo_end(b):
+        @pl.when(permutes)
+        def _():
+            fold(b)
+
+    def south_in(b):
         @pl.when(has_south)
         def _():
             arrived(south.at[b], r_halo.at[b, 0])
@@ -367,6 +362,7 @@
             south[b] = jnp.zeros((3, 192, 128), BF)
             diff_s[b] = jnp.zeros((192, 128), F32)
 
+    def north_in(b):
         @pl.when(has_north)
         def _():
             arrived(north.at[b, 0], r_halo.at[b, 1])
@@ -374,10 +370,7 @@
 
         @pl.when(on_line)
         def _():
-            for p in range(GROUPS):
-                @pl.when(line != p)
-                def _():
-                    arrived(north.at[b, :, :, pl.ds(p * 16, 16), :], r_f3.at[b, p])
+            arrived(north.at[b], r_f3.at[b])
 
             @pl.loop(0, GROUPS)
             def _(g):
@@ -403,57 +396,42 @@
 
         @pl.when(on_line)
         def _():
-            for p in range(GROUPS):
-                @pl.when(line != p)
-                def _():
-                    rim_copy(b, p).wait_send()
-
-            @pl.when(line < GROUPS)
-            def _():
-                for j in range(16):
-                    @pl.when(col_block != j)
-                    def _():
-                        ghost_copy(b, j).wait_send()
-
-    def depthwise(b, inner):
-        spans = ((3, 13),) if inner else ((0, 3), (13, 16))
-
+            rim = state.at[b, pl.ds(13, 3)]
+            remote(rim, rim, s_f1.at[b], r_f1.at[b], far).wait_send()
+
+        @pl.when(permutes)
+        def _():
+            remote(fold_out.at[b], fold_out.at[b], s_f3.at[b], r_f3.at[b], far).wait_send()
+
+    def depthwise(b, lo, hi):
         @pl.loop(0, GROUPS)
         def _(g):
             ch = group(g)
-            if not inner:
-                for r in range(3):
+            for r in range(3):
+                if lo == 0:
                     xrow[r, ch, :] = south[b, r, ch, :].astype(F32)
+                if hi == 16:
                     xrow[r + 19, ch, :] = north[b, 0, r, ch, :].astype(F32)
-            xs = {r: xrow[r, ch, :] for lo, hi in spans for r in range(lo, hi + 6)}
+            xs = {r: xrow[r, ch, :] for r in range(lo, hi + 6)}
             acc = {}
             for e in range(7):
                 w = [taps[b, a * 7 + e, ch, :] for a in range(7)]
-                for lo, hi in spans:
-                    for q in range(lo, hi):
-                        v = w[0] * xs[q]
-                        for a in range(1, 7):
-                            v = v + w[a] * xs[q + a]
-                        if e != 3:
-                            v = pltpu.roll(v, (3 - e) % 128, 1)
-                        acc[q] = v if e == 0 else acc[q] + v
+                for q in range(lo, hi):
+                    v = w[0] * xs[q]
+                    for a in range(1, 7):
+                        v = v + w[a] * xs[q + a]
+                    if e != 3:
+                        v = pltpu.roll(v, (3 - e) % 128, 1)
+                    acc[q] = v if e == 0 else acc[q] + v
             for q in acc:
                 conv[q, ch, :] = acc[q]
 
-    def correct(b, inner):
+    def correct(b, lo, hi):
         tile = diff[b]
-        rows = [(q, q - 3) for q in range(3, 13)]
-        if not inner:
-            tile = jnp.where(
-                wide_lane < 18,
-                pltpu.roll(diff_s[b], 50, 1),
-                jnp.where(
-                    wide_lane < 54,
-                    pltpu.roll(tile, 18, 1),
-                    jnp.where(wide_lane < 90, pltpu.roll(tile, 122, 1), pltpu.roll(diff_n[b], 90, 1)),
-                ),
-            )
-            rows = [(0, 0), (1, 1), (2, 2), (13, 9), (14, 10), (15, 11)]
+        if lo == 0:
+            tile = jnp.where(wide_lane < 18, pltpu.roll(diff_s[b], 50, 1), pltpu.roll(tile, 18, 1))
+        elif hi == 16:
+            tile = jnp.where(wide_lane < 36, pltpu.roll(tile, 68, 1), pltpu.roll(diff_n[b], 36, 1))
         sums = [None] * 3
         for a in range(7):
             moved = pltpu.roll(tile, (-6 * a) % 128, 1) if a else tile
@@ -465,49 +443,55 @@
         fix = fix + jnp.where(~west_slot & (place >= 1), pltpu.roll(sums[1], 1, 1), 0.0)
         fix = fix + jnp.where(west_slot & (place == 0), pltpu.roll(sums[2], 126, 1), 0.0)
         fix = fix + jnp.where(~west_slot & (place == 2), pltpu.roll(sums[0], 2, 1), 0.0)
-        for q, k in rows:
-            conv[q] += jnp.where(row_ends, pltpu.roll(fix, (-6 * k - 3) % 128, 1), 0.0)
+        for q in range(lo, hi):
+            conv[q] += jnp.where(row_ends, pltpu.roll(fix, (-6 * (q - lo) - 3) % 128, 1), 0.0)
 
     def pointwise(b, first):
-        @pl.loop(0, 2)
-        def _(n):
-            for q in range(2):
-                i = first(n) + q
-                parts = []
-                for k in range(2):
-                    cv = conv[2 * i + k]
-                    mu = jnp.sum(cv, axis=0, keepdims=True) * (1.0 / 192)
-                    var = jnp.sum(cv * cv, axis=0, keepdims=True) * (1.0 / 192) - mu * mu
-                    parts.append(((cv - mu) * lax.rsqrt(var + 1e-6) * gain[b]).astype(BF))
-                normed = jnp.concatenate(parts, axis=1)
-                branch = jnp.zeros((192, 256), F32)
-                for side, w in enumerate((w_own, w_other)):
-                    pre = jnp.dot(w[2 * b].reshape(384, 192), normed, preferred_element_type=F32)
-                    hidden = twice_gelu(pre).astype(BF)
-                    branch = branch + jnp.dot(down_t[b, side], hidden, preferred_element_type=F32)
-                for k in range(2):
-                    r = 2 * i + k
-                    new = (state[b, r].astype(F32) + 0.5 * branch[:, k * 128 : (k + 1) * 128]) * sea_rows(r)
-                    if b == 0:
-                        state[1, r] = new.astype(BF)
-                    else:
-                        out_f[pl.ds(r, 192, stride=16), :] = new
+        for q in range(2):
+            i = first + q
+            parts = []
+            for k in range(2):
+                cv = conv[2 * i + k]
+                mu = jnp.sum(cv, axis=0, keepdims=True) * (1.0 / 192)
+                var = jnp.sum(cv * cv, axis=0, keepdims=True) * (1.0 / 192) - mu * mu
+                parts.append(((cv - mu) * lax.rsqrt(var + 1e-6) * gain[b]).astype(BF))
+            normed = jnp.concatenate(parts, axis=1)
+            branch = jnp.zeros((192, 256), F32)
+            for side, w in enumerate((w_own, w_other)):
+                pre = jnp.dot(w[2 * b].reshape(384, 192), normed, preferred_element_type=F32)
+                hidden = twice_gelu(pre).astype(BF)
+                branch = branch + jnp.dot(down_t[b, side], hidden, preferred_element_type=F32)
+            for k in range(2):
+                r = 2 * i + k
+                new = (state[b, r].astype(F32) + 0.5 * branch[:, k * 128 : (k + 1) * 128]) * sea_rows(r)
+                if b == 0:
+                    state[1, r] = new.astype(BF)
+                else:
+                    out_f[pl.ds(r, 192, stride=16), :] = new
 
     for b in range(2):
         halo_start(b)
-        depthwise(b, True)
+        depthwise(b, 3, 13)
         if b == 0:
             arrived(w_other, r_w.at[14])
             for bb in range(2):
                 for side, w in enumerate((w_own, w_other)):
                     down_t[bb, side] = w[2 * bb + 1].reshape(384, 192).astype(F32).T.astype(BF)
         halo_middle(b)
-        correct(b, True)
-        pointwise(b, lambda n: 2 + 2 * n)
-        halo_end(b)
-        depthwise(b, False)
-        correct(b, False)
-        pointwise(b, lambda n: 6 * n)
+        correct(b, 3, 13)
+
+        @pl.loop(0, 2)
+        def _(n):
+            pointwise(b, 2 + 2 * n)
+
+        south_in(b)
+        depthwise(b, 0, 3)
+        correct(b, 0, 3)
+        pointwise(b, 0)
+        north_in(b)
+        depthwise(b, 13, 16)
+        correct(b, 13, 16)
+        pointwise(b, 6)
 
     def chunk(l):
         chans = pl.ds(l * 24, 24)
@@ -566,17 +550,17 @@
         pltpu.VMEM((2, 192, 128), BF),
         pltpu.VMEM((2, 192, 128), BF),
         pltpu.VMEM((22, 192, 128), F32),
-        pltpu.VMEM((8, 2048, 256), BF),
-        pltpu.VMEM((2, 16, 3, 16, 128), BF),
-        pltpu.VMEM((2, 16, 2, 3, 16, 128), BF),
+        pltpu.VMEM((2, 16, 16, 128), BF),
+        pltpu.VMEM((2, 16, 2, 16, 128), BF),
+        pltpu.VMEM((16, 16, 128), F32),
         pltpu.VMEM((192 * 16, 128), F32),
         pltpu.VMEM((192, 16, 128), BF),
         dma((7,)), dma((8,)),
         dma((7,)),
         dma((12,)), dma((15,)),
         dma((2, 6)), dma((2, 6)),
-        dma((2, 12)), dma((2, 16)),
-        dma((2, 16)), dma((2, 12)),
+        dma((2,)), dma((2,)),
+        dma((2,)), dma((2,)),
         dma((8,)), dma((8,)),
     ]
     return pl.pallas_call(

time: 121 us -> 118 us (0.975)
  the two profiles are of different devices: /device:TPU:127 before, /device:TPU:62 now
where the time goes in v4:
time: 118 us
  Pallas kernels  114 us (97%)
  local copies, waits for them, and re-layouts  3.72 us (3%)
    pallas_call x1, Pallas kernels, body(): pl.pallas_call(kernel, out_shape=jax.ShapeDtypeStruct((24, 64, 256), BF),...  114 us
    unnamed x2, local copies, waits for them, and re-layouts  3.72 us

profile of v4, /device:TPU:62, one launch (start us, length us, event | category | flops | bytes accessed | tf_op | source)
XLA Modules:
  0.0 118.2 jit_solution(8001917869226813599)
XLA Ops:
  0.0 1.6 %copy.9.dw_weight = f32[2,24,7,7]{3,2,1,0:T(8,128)} copy(f32[2,24,7,7]{1,0,3,2:T(2,128)} %param.12) | data formatting | bytes 18816 | tf_op args[4]
  1.6 114.4 %shard_map.82 = bf16[24,64,256]{2,1,0:T(8,128)(2,1)} custom-call(bf16[40,64,256]{2,1,0:T(8,128)(2,1)} %fields.1, s32[64,256]{1,0:T(8,128)} %sea.1, s32[16,128]{1,0:T(8,128)} %bitcast.1, bf16[40,192]{1,0:T(8,128)(2,1)} %embed.1, f32[2,24,7,7]{3,2,1,0:T(8,128)} %copy.9.dw_weight, bf16[2,24]{1,0:T(2,128)(2,1)} %ln_gain.1, bf16[2,96,192]{2,1,0:T(8,128)(2,1)} %up.1, ...), custom_call_target="tpu_custom_call" | custom-call | tf_op jit(solution)/shard_map/pallas_call | solution.py:566
  116.1 2.1 %copy.11 = bf16[24,64,256]{2,1,0:T(8,128)(2,1)} copy(bf16[24,64,256]{2,1,0:T(8,128)(2,1)} %shard_map.82) | data formatting | bytes 1572864

commit v5 on v4

--- a/solution.py
+++ b/solution.py
@@ -281,6 +281,12 @@
             remote(diff.at[b], diff_n.at[b], s_halo.at[b, 5], r_halo.at[b, 5], south_dev),
         )
 
+    def pack_copies(b):
+        return (
+            remote(pack.at[b], from_w.at[b], s_halo.at[b, 2], r_halo.at[b, 2], east),
+            remote(pack.at[b], from_e.at[b], s_halo.at[b, 3], r_halo.at[b, 3], west),
+        )
+
     def start_pair(pair):
         @pl.when(has_north)
         def _():
@@ -311,8 +317,8 @@
                 tile = jnp.where((lane96 >= 6 * r) & (lane96 < 6 * r + 6), pltpu.roll(v, 6 * r + 3, 1), tile)
             pack[b, ch, :] = tile.astype(BF)
 
-        send(pack.at[b], from_w.at[b], s_halo.at[b, 2], r_halo.at[b, 2], east)
-        send(pack.at[b], from_e.at[b], s_halo.at[b, 3], r_halo.at[b, 3], west)
+        for cp in pack_copies(b):
+            cp.start()
 
     def fold(b):
         arrived(fold_in.at[b], r_f1.at[b])
@@ -385,6 +391,9 @@
                 diff_n[b, ch, :] = tile
 
     def halo_sent(b):
+        for cp in pack_copies(b):
+            cp.wait_send()
+
         for pair in (row_copies(b), side_copies(b)):
             @pl.when(has_north)
             def _():
@@ -464,19 +473,21 @@
             for k in range(2):
                 r = 2 * i + k
                 new = (state[b, r].astype(F32) + 0.5 * branch[:, k * 128 : (k + 1) * 128]) * sea_rows(r)
-                if b == 0:
-                    state[1, r] = new.astype(BF)
-                else:
-                    out_f[pl.ds(r, 192, stride=16), :] = new
-
-    for b in range(2):
+                state[b + 1, r] = new.astype(BF)
+                out_f[pl.ds(r, 192, stride=16), :] = new
+
+    @pl.loop(0, 2)
+    def _(b):
         halo_start(b)
         depthwise(b, 3, 13)
-        if b == 0:
+
+        @pl.when(b == 0)
+        def _():
             arrived(w_other, r_w.at[14])
-            for bb in range(2):
-                for side, w in enumerate((w_own, w_other)):
-                    down_t[bb, side] = w[2 * bb + 1].reshape(384, 192).astype(F32).T.astype(BF)
+
+        for side, w in enumerate((w_own, w_other)):
+            down_t[b, side] = w[2 * b + 1].reshape(384, 192).astype(F32).T.astype(BF)
+
         halo_middle(b)
         correct(b, 3, 13)
 
@@ -512,7 +523,8 @@
     last.wait()
     for cp in sends:
         cp.wait_send()
-    for b in range(2):
+    @pl.loop(0, 2)
+    def _(b):
         halo_sent(b)
 
 
@@ -540,7 +552,7 @@
         pltpu.VMEM((2, 2, 192, 384), BF),
         pltpu.VMEM((2, 192, 128), F32),
         pltpu.VMEM((16, 192, 128), F32),
-        pltpu.VMEM((2, 16, 192, 128), BF),
+        pltpu.VMEM((3, 16, 192, 128), BF),
         pltpu.VMEM((2, 3, 192, 128), BF),
         pltpu.VMEM((2, 2, 3, 192, 128), BF),
         pltpu.VMEM((2, 192, 128), F32),

time: 118 us -> 111 us (0.941)
  the two profiles are of different devices: /device:TPU:62 before, /device:TPU:127 now
where the time goes in v5:
time: 111 us; the launch traced here: 110 us
  Pallas kernels  106 us (95%)
  local copies, waits for them, and re-layouts  3.72 us (3%)
    pallas_call x1, Pallas kernels, body(): pl.pallas_call(kernel, out_shape=jax.ShapeDtypeStruct((24, 64, 256), BF),...  106 us
    unnamed x2, local copies, waits for them, and re-layouts  3.72 us

profile of v5, /device:TPU:127, one launch (start us, length us, event | category | flops | bytes accessed | tf_op | source)
XLA Modules:
  0.0 109.8 jit_solution(12171720889805353769)
XLA Ops:
  0.0 1.6 %copy.9.dw_weight = f32[2,24,7,7]{3,2,1,0:T(8,128)} copy(f32[2,24,7,7]{1,0,3,2:T(2,128)} %param.12) | data formatting | bytes 18816 | tf_op args[4]
  1.6 106.1 %shard_map.82 = bf16[24,64,256]{2,1,0:T(8,128)(2,1)} custom-call(bf16[40,64,256]{2,1,0:T(8,128)(2,1)} %fields.1, s32[64,256]{1,0:T(8,128)} %sea.1, s32[16,128]{1,0:T(8,128)} %bitcast.1, bf16[40,192]{1,0:T(8,128)(2,1)} %embed.1, f32[2,24,7,7]{3,2,1,0:T(8,128)} %copy.9.dw_weight, bf16[2,24]{1,0:T(2,128)(2,1)} %ln_gain.1, bf16[2,96,192]{2,1,0:T(8,128)(2,1)} %up.1, ...), custom_call_target="tpu_custom_call" | custom-call | tf_op jit(solution)/shard_map/pallas_call | solution.py:578
  107.7 2.1 %copy.11 = bf16[24,64,256]{2,1,0:T(8,128)(2,1)} copy(bf16[24,64,256]{2,1,0:T(8,128)(2,1)} %shard_map.82) | data formatting | bytes 1572864

commit v6 on v5

--- a/solution.py
+++ b/solution.py
@@ -21,8 +21,8 @@
     out,
     x_in, sea_in, partner_in, embed_in, dw_raw, gain_raw,
     xt, flat, pe, dw_in, dw_all, taps, end_taps, emb_t, w_own, w_other, down_t, gain, conv,
-    state, south, north, diff, diff_s, diff_n, pack, from_w, from_e, xrow,
-    fold_in, fold_out, fold_src, out_f, out_b,
+    state, south, north, diff, diff_s, diff_n, pack, from_w, from_e, xrow, edge_tile,
+    fold_in, fold_out, fold_src, out_f, out_b, out_in,
     s_x, r_x, s_loc, s_w, r_w, s_halo, r_halo, s_f1, r_f1, s_f3, r_f3, s_o, r_o,
 ):
     lev = lax.axis_index("lev")
@@ -150,11 +150,10 @@
     diagonal = lax.broadcasted_iota(jnp.int32, (24, 24), 0) == lax.broadcasted_iota(jnp.int32, (24, 24), 1)
     gains = gain_raw[...].astype(F32)
     for b in range(2):
-        raw = dw_raw[b]
+        raw = jnp.concatenate([dw_raw[:, b, :], jnp.zeros((49, 104), F32)], axis=1)
+        by_channel = jnp.concatenate([raw, jnp.zeros((79, 128), F32)], axis=0).T[:24, :]
         column = jnp.sum(jnp.where(diagonal, gains[b : b + 1, :], 0.0), axis=1, keepdims=True)
-        dslot[b] = jnp.concatenate(
-            [raw[:, a, :] for a in range(7)] + [column, jnp.zeros((24, 78), F32)], axis=1
-        )
+        dslot[b] = jnp.where(lax.broadcasted_iota(jnp.int32, (24, 128), 1) == 49, column, by_channel)
     pltpu.make_async_copy(up.at[0].at[half_rows, :], slot.at[0], s_loc.at[0]).wait()
 
     across = jnp.where(on_line, jnp.where(gx < 6, 30, 36), jnp.where(permutes, 14, 0))
@@ -238,15 +237,6 @@
     def sea_rows(r):
         return sea_in[pl.ds(r, 1), :].astype(F32)
 
-    @pl.loop(0, 4)
-    def _(n):
-        for q in range(2):
-            r = 4 * n + 2 * q
-            both = jnp.concatenate([xt[r], xt[r + 1]], axis=1)
-            stem = jnp.dot(emb_t[...], both, preferred_element_type=F32)
-            state[0, r] = (stem[:, :128] * sea_rows(r)).astype(BF)
-            state[0, r + 1] = (stem[:, 128:] * sea_rows(r + 1)).astype(BF)
-
     lane = lax.broadcasted_iota(jnp.int32, (16, 128), 1)
 
     wide_lane = lax.broadcasted_iota(jnp.int32, (192, 128), 1)
@@ -257,16 +247,16 @@
     def group(g):
         return pl.ds(pl.multiple_of(g * 16, 16), 16)
 
-    def rim_copy(b, k, p):
+    def rim_copy(b, k, tp, q):
         return remote(
-            state.at[b, 15 - k, group(p), :], fold_in.at[b, col_block], s_f1.at[b], r_f1.at[b], permuter(k, p)
-        )
-
-    def ghost_copy(b, j):
-        tj, cj, sj = j // 4, lax.rem(j // 2, 2), lax.rem(j, 2)
+            state.at[b, 15 - k, group(tp * 4 + q), :], fold_in.at[b, col_block],
+            s_f1.at[b], r_f1.at[b], device(x, 1 + k, q % 2, tp, q // 2),
+        )
+
+    def ghost_copy(b, kind, tj, q):
         return remote(
-            fold_out.at[b, j], north.at[b, :, y - 1, group(line), :],
-            s_f3.at[b], r_f3.at[b], device(x, 0, lax.rem(sj + cj, 2), tj, cj),
+            fold_out.at[b, kind, tj * 4 + q], north.at[b, kind, y - 1, group(line), :],
+            s_f3.at[b, kind], r_f3.at[b, kind], device(x, 0, (q % 2) ^ (q // 2), tj, q // 2),
         )
 
     def row_copies(b):
@@ -296,16 +286,16 @@
         def _():
             pair[1].start()
 
+    def rim_start(b):
+        @pl.when(on_line)
+        def _():
+            @pl.loop(0, 3)
+            def _(tp):
+                for q in range(4):
+                    for k in range(3):
+                        rim_copy(b, k, tp, q).start()
+
     def halo_start(b):
-        @pl.when(on_line)
-        def _():
-            @pl.loop(0, GROUPS)
-            def _(p):
-                for k in range(3):
-                    rim_copy(b, k, p).start()
-
-        start_pair(row_copies(b))
-
         @pl.loop(0, 2)
         def _(g):
             ch = pl.ds(pl.multiple_of(g * 96, 96), 96)
@@ -319,30 +309,39 @@
 
         for cp in pack_copies(b):
             cp.start()
+        start_pair(row_copies(b))
 
     def fold(b):
         arrived(fold_in.at[b], r_f1.at[b])
         for j in range(16):
             fold_src[j] = fold_in[b, j].astype(F32)
 
-        ghosts = []
+        @pl.loop(0, 4)
+        def _(tj):
+            for q in range(4):
+                column = jnp.broadcast_to(partner_in[pl.ds(tj * 4 + q, 1), :], (16, 128))
+                within, block = column & 127, column >> 7
+                picked = [jnp.take_along_axis(fold_src[i], within, axis=1) for i in range(16)]
+                for bit in range(4):
+                    odd = ((block >> bit) & 1) == 1
+                    picked = [jnp.where(odd, picked[i + 1], picked[i]) for i in range(0, len(picked), 2)]
+                fold_out[b, 0, tj * 4 + q] = picked[0].astype(BF)
+                ghost_copy(b, 0, tj, q).start()
+
         for j in range(16):
-            column = jnp.broadcast_to(partner_in[j : j + 1, :], (16, 128))
-            within, block = column & 127, column >> 7
-            picked = [jnp.take_along_axis(fold_src[i], within, axis=1) for i in range(16)]
-            for bit in range(4):
-                odd = ((block >> bit) & 1) == 1
-                picked = [jnp.where(odd, picked[i + 1], picked[i]) for i in range(0, len(picked), 2)]
-            ghosts.append(picked[0])
-        for j in range(16):
-            fold_out[b, j, 0] = ghosts[j].astype(BF)
-            fold_out[b, j, 1] = jnp.where(lane < 64, ghosts[(j + 1) % 16], ghosts[j - 1]).astype(BF)
-
-        @pl.loop(0, 16)
-        def _(j):
-            ghost_copy(b, j).start()
+            after, before = fold_out[b, 0, (j + 1) % 16], fold_out[b, 0, (j + 15) % 16]
+            fold_out[b, 1, j] = jnp.where(lane < 64, after.astype(F32), before.astype(F32)).astype(BF)
+
+        @pl.loop(0, 4)
+        def _(tj):
+            for q in range(4):
+                ghost_copy(b, 1, tj, q).start()
 
     def halo_middle(b):
+        @pl.when(permutes)
+        def _():
+            fold(b)
+
         arrived(from_w.at[b], r_halo.at[b, 2])
         arrived(from_e.at[b], r_halo.at[b, 3])
         mine = pack[b].astype(F32)
@@ -353,30 +352,41 @@
         )
         start_pair(side_copies(b))
 
-        @pl.when(permutes)
-        def _():
-            fold(b)
-
     def south_in(b):
         @pl.when(has_south)
         def _():
             arrived(south.at[b], r_halo.at[b, 0])
+
+        @pl.when(jnp.logical_not(has_south))
+        def _():
+            south[b] = jnp.zeros((3, 192, 128), BF)
+
+    def south_sides_in(b):
+        @pl.when(has_south)
+        def _():
             arrived(diff_s.at[b], r_halo.at[b, 4])
 
         @pl.when(jnp.logical_not(has_south))
         def _():
-            south[b] = jnp.zeros((3, 192, 128), BF)
             diff_s[b] = jnp.zeros((192, 128), F32)
 
     def north_in(b):
         @pl.when(has_north)
         def _():
             arrived(north.at[b, 0], r_halo.at[b, 1])
+
+        @pl.when(on_line)
+        def _():
+            arrived(north.at[b, 0], r_f3.at[b, 0])
+
+    def north_sides_in(b):
+        @pl.when(has_north)
+        def _():
             arrived(diff_n.at[b], r_halo.at[b, 5])
 
         @pl.when(on_line)
         def _():
-            arrived(north.at[b], r_f3.at[b])
+            arrived(north.at[b, 1], r_f3.at[b, 1])
 
             @pl.loop(0, GROUPS)
             def _(g):
@@ -410,22 +420,19 @@
 
         @pl.when(permutes)
         def _():
-            remote(fold_out.at[b], fold_out.at[b], s_f3.at[b], r_f3.at[b], far).wait_send()
-
-    def depthwise(b, lo, hi):
+            for kind in range(2):
+                done = fold_out.at[b, kind]
+                remote(done, done, s_f3.at[b, kind], r_f3.at[b, kind], far).wait_send()
+
+    def depthwise(b, lo, count):
         @pl.loop(0, GROUPS)
         def _(g):
             ch = group(g)
-            for r in range(3):
-                if lo == 0:
-                    xrow[r, ch, :] = south[b, r, ch, :].astype(F32)
-                if hi == 16:
-                    xrow[r + 19, ch, :] = north[b, 0, r, ch, :].astype(F32)
-            xs = {r: xrow[r, ch, :] for r in range(lo, hi + 6)}
+            xs = [xrow[lo + r, ch, :] for r in range(count + 6)]
             acc = {}
             for e in range(7):
                 w = [taps[b, a * 7 + e, ch, :] for a in range(7)]
-                for q in range(lo, hi):
+                for q in range(count):
                     v = w[0] * xs[q]
                     for a in range(1, 7):
                         v = v + w[a] * xs[q + a]
@@ -433,14 +440,9 @@
                         v = pltpu.roll(v, (3 - e) % 128, 1)
                     acc[q] = v if e == 0 else acc[q] + v
             for q in acc:
-                conv[q, ch, :] = acc[q]
-
-    def correct(b, lo, hi):
-        tile = diff[b]
-        if lo == 0:
-            tile = jnp.where(wide_lane < 18, pltpu.roll(diff_s[b], 50, 1), pltpu.roll(tile, 18, 1))
-        elif hi == 16:
-            tile = jnp.where(wide_lane < 36, pltpu.roll(tile, 68, 1), pltpu.roll(diff_n[b], 36, 1))
+                conv[lo + q, ch, :] = acc[q]
+
+    def correct(b, tile, lo, count):
         sums = [None] * 3
         for a in range(7):
             moved = pltpu.roll(tile, (-6 * a) % 128, 1) if a else tile
@@ -452,34 +454,65 @@
         fix = fix + jnp.where(~west_slot & (place >= 1), pltpu.roll(sums[1], 1, 1), 0.0)
         fix = fix + jnp.where(west_slot & (place == 0), pltpu.roll(sums[2], 126, 1), 0.0)
         fix = fix + jnp.where(~west_slot & (place == 2), pltpu.roll(sums[0], 2, 1), 0.0)
-        for q in range(lo, hi):
-            conv[q] += jnp.where(row_ends, pltpu.roll(fix, (-6 * (q - lo) - 3) % 128, 1), 0.0)
-
-    def pointwise(b, first):
+        for q in range(count):
+            conv[lo + q] += jnp.where(row_ends, pltpu.roll(fix, (-6 * q - 3) % 128, 1), 0.0)
+
+    def pointwise(b, first, part):
+        parts = []
+        for k in range(4):
+            cv = conv[2 * first + k]
+            mu = jnp.sum(cv, axis=0, keepdims=True) * (1.0 / 192)
+            var = jnp.sum(cv * cv, axis=0, keepdims=True) * (1.0 / 192) - mu * mu
+            parts.append(((cv - mu) * lax.rsqrt(var + 1e-6) * gain[b]).astype(BF))
+        normed = jnp.concatenate(parts, axis=1)
+        branch = jnp.zeros((192, 512), F32)
+        for side, w in enumerate((w_own, w_other)):
+            pre = jnp.dot(w[2 * b].reshape(384, 192), normed, preferred_element_type=F32)
+            hidden = twice_gelu(pre.astype(BF))
+            branch = branch + jnp.dot(down_t[b, side], hidden, preferred_element_type=F32)
+        for k in range(4):
+            r = 2 * first + k
+            new = (state[b, r].astype(F32) + 0.5 * branch[:, k * 128 : (k + 1) * 128]) * sea_rows(r)
+            state[b + 1, r] = new.astype(BF)
+            out_f[pl.ds(part * 1536 + lax.rem(r, 8), 192, stride=8), :] = new
+
+    def out_copy(part, i):
+        k, flip = others[i]
+        hh = lax.rem(h + flip, 2)
+        chans = pl.ds((ys[k] * 2 + hh) * 12, 12)
+        return remote(
+            out_b.at[part, chans], out_in.at[part, lev], s_o.at[part, i], r_o.at[part, lev],
+            device(x, ys[k], hh, t, c),
+        )
+
+    def out_start(part):
+        def fill(l):
+            rows = out_f[pl.ds(pl.multiple_of(part * 1536 + l * 192, 192), 192), :]
+            out_b[part, pl.ds(l * 12, 12)] = rows.reshape(12, 16, 128).astype(BF)
+
+        for i, (k, flip) in enumerate(others):
+            fill(ys[k] * 2 + lax.rem(h + flip, 2))
+            out_copy(part, i).start()
+        fill(lev)
+        out_in[part, lev] = out_b[part, pl.ds(lev * 12, 12)]
+
+    @pl.loop(0, 4)
+    def _(n):
         for q in range(2):
-            i = first + q
-            parts = []
-            for k in range(2):
-                cv = conv[2 * i + k]
-                mu = jnp.sum(cv, axis=0, keepdims=True) * (1.0 / 192)
-                var = jnp.sum(cv * cv, axis=0, keepdims=True) * (1.0 / 192) - mu * mu
-                parts.append(((cv - mu) * lax.rsqrt(var + 1e-6) * gain[b]).astype(BF))
-            normed = jnp.concatenate(parts, axis=1)
-            branch = jnp.zeros((192, 256), F32)
-            for side, w in enumerate((w_own, w_other)):
-                pre = jnp.dot(w[2 * b].reshape(384, 192), normed, preferred_element_type=F32)
-                hidden = twice_gelu(pre).astype(BF)
-                branch = branch + jnp.dot(down_t[b, side], hidden, preferred_element_type=F32)
-            for k in range(2):
-                r = 2 * i + k
-                new = (state[b, r].astype(F32) + 0.5 * branch[:, k * 128 : (k + 1) * 128]) * sea_rows(r)
-                state[b + 1, r] = new.astype(BF)
-                out_f[pl.ds(r, 192, stride=16), :] = new
+            r = 12 - 4 * n + 2 * q
+            both = jnp.concatenate([xt[r], xt[r + 1]], axis=1)
+            stem = jnp.dot(emb_t[...], both, preferred_element_type=F32)
+            state[0, r] = (stem[:, :128] * sea_rows(r)).astype(BF)
+            state[0, r + 1] = (stem[:, 128:] * sea_rows(r + 1)).astype(BF)
+
+        @pl.when(n == 0)
+        def _():
+            rim_start(0)
 
     @pl.loop(0, 2)
     def _(b):
         halo_start(b)
-        depthwise(b, 3, 13)
+        depthwise(b, 3, 10)
 
         @pl.when(b == 0)
         def _():
@@ -489,38 +522,70 @@
             down_t[b, side] = w[2 * b + 1].reshape(384, 192).astype(F32).T.astype(BF)
 
         halo_middle(b)
-        correct(b, 3, 13)
-
-        @pl.loop(0, 2)
-        def _(n):
-            pointwise(b, 2 + 2 * n)
-
-        south_in(b)
-        depthwise(b, 0, 3)
-        correct(b, 0, 3)
-        pointwise(b, 0)
-        north_in(b)
-        depthwise(b, 13, 16)
-        correct(b, 13, 16)
-        pointwise(b, 6)
-
-    def chunk(l):
-        chans = pl.ds(l * 24, 24)
-        out_b[chans] = out_f[pl.ds(pl.multiple_of(l * 384, 384), 384), :].reshape(24, 16, 128).astype(BF)
-        return out_b.at[chans]
-
-    for i, (k, flip) in enumerate(others):
+
+        @pl.loop(0, 3)
+        def _(phase):
+            @pl.when(phase == 0)
+            def _():
+                correct(b, diff[b], 3, 10)
+
+            @pl.when(phase == 1)
+            def _():
+                south_in(b)
+                xrow[0:3] = south[b].astype(F32)
+
+            @pl.when(phase == 2)
+            def _():
+                north_in(b)
+                xrow[19:22] = north[b, 0].astype(F32)
+
+            @pl.when(phase > 0)
+            def _():
+                lo = 13 * (phase - 1)
+                depthwise(b, lo, 3)
+
+                @pl.when(phase == 1)
+                def _():
+                    south_sides_in(b)
+                    below = pltpu.roll(diff_s[b], 50, 1)
+                    edge_tile[...] = jnp.where(wide_lane < 18, below, pltpu.roll(diff[b], 18, 1))
+
+                @pl.when(phase == 2)
+                def _():
+                    north_sides_in(b)
+                    above = pltpu.roll(diff_n[b], 36, 1)
+                    edge_tile[...] = jnp.where(wide_lane < 36, pltpu.roll(diff[b], 68, 1), above)
+
+                correct(b, edge_tile[...], lo, 3)
+
+            @pl.loop(0, jnp.where(phase == 0, 2, 1))
+            def _(n):
+                pointwise(b, jnp.where(phase == 0, 2 + 2 * n, 6 * (phase - 1)), jnp.where(phase == 0, 0, 1))
+
+            @pl.when((b == 0) & (phase == 2))
+            def _():
+                rim_start(1)
+
+            @pl.when((b == 1) & (phase != 1))
+            def _():
+                out_start(phase // 2)
+
+    upper = lax.broadcasted_iota(jnp.int32, (24, 8, 128), 1) < 4
+    for k, flip in [(0, 0)] + others[4:] + others[:4]:
         hh = lax.rem(h + flip, 2)
-        send(
-            chunk(ys[k] * 2 + hh), out.at[:, my_rows, my_cols], s_o.at[i], r_o.at[lev], device(x, ys[k], hh, t, c)
-        )
-    last = pltpu.make_async_copy(chunk(lev), out.at[:, my_rows, my_cols], s_o.at[7])
-    last.start()
-    for k, flip in others:
-        hh = lax.rem(h + flip, 2)
+        l = ys[k] * 2 + hh
+        if (k, flip) != (0, 0):
+            for part in range(2):
+                arrived(out_in.at[part, l], r_o.at[part, l])
+        mid = out_in[0, l].astype(F32).reshape(24, 8, 128)
+        rim = out_in[1, l].astype(F32).reshape(24, 8, 128)
         rows, cols = cells_of(ys[k], hh)
-        arrived(out.at[:, rows, cols], r_o.at[ys[k] * 2 + hh])
-    last.wait()
+        out[:, rows, cols] = jnp.concatenate(
+            [jnp.where(upper, rim, mid), jnp.where(upper, mid, rim)], axis=1
+        ).astype(BF)
+    for part in range(2):
+        for i in range(7):
+            out_copy(part, i).wait_send()
     for cp in sends:
         cp.wait_send()
     @pl.loop(0, 2)
@@ -530,6 +595,7 @@
 
 def body(fields, sea_mask, fold_partner, embed_weight, dw_weight, ln_gain, up_weight, down_weight):
     partner = fold_partner.reshape(16, 128)
+    by_tap = jnp.transpose(dw_weight, (2, 3, 0, 1)).reshape(49, 2, 24)
     hbm = pl.BlockSpec(memory_space=pl.ANY)
     dma = pltpu.SemaphoreType.DMA
     scratch = [
@@ -537,7 +603,7 @@
         pltpu.VMEM((16, 128), jnp.int32),
         pltpu.VMEM((16, 128), jnp.int32),
         pltpu.VMEM((40, 192), BF),
-        pltpu.VMEM((2, 24, 7, 7), F32),
+        pltpu.VMEM((49, 2, 24), F32),
         pltpu.VMEM((2, 24), BF),
         pltpu.VMEM((16, 384, 128), BF),
         pltpu.VMEM((640, 128), F32),
@@ -562,29 +628,31 @@
         pltpu.VMEM((2, 192, 128), BF),
         pltpu.VMEM((2, 192, 128), BF),
         pltpu.VMEM((22, 192, 128), F32),
+        pltpu.VMEM((192, 128), F32),
         pltpu.VMEM((2, 16, 16, 128), BF),
-        pltpu.VMEM((2, 16, 2, 16, 128), BF),
+        pltpu.VMEM((2, 2, 16, 16, 128), BF),
         pltpu.VMEM((16, 16, 128), F32),
         pltpu.VMEM((192 * 16, 128), F32),
-        pltpu.VMEM((192, 16, 128), BF),
+        pltpu.VMEM((2, 96, 16, 128), BF),
+        pltpu.VMEM((2, 8, 12, 16, 128), BF),
         dma((7,)), dma((8,)),
         dma((7,)),
         dma((12,)), dma((15,)),
         dma((2, 6)), dma((2, 6)),
         dma((2,)), dma((2,)),
-        dma((2,)), dma((2,)),
-        dma((8,)), dma((8,)),
+        dma((2, 2)), dma((2, 2)),
+        dma((2, 7)), dma((2, 8)),
     ]
     return pl.pallas_call(
         kernel,
         out_shape=jax.ShapeDtypeStruct((24, 64, 256), BF),
         in_specs=[hbm] * 8,
-        out_specs=hbm,
+        out_specs=pl.BlockSpec(memory_space=pltpu.VMEM),
         scratch_shapes=scratch,
         compiler_params=pltpu.CompilerParams(
             collective_id=0, has_side_effects=True, vmem_limit_bytes=60 * 1024 * 1024
         ),
-    )(fields, sea_mask, partner, embed_weight, dw_weight, ln_gain, up_weight, down_weight)
+    )(fields, sea_mask, partner, embed_weight, by_tap, ln_gain, up_weight, down_weight)
 
 
 def solution(mesh):

time: 111 us -> 104 us (0.937)
  Pallas kernels: 106 us -> 102 us
  local copies, waits for them, and re-layouts: 3.72 us -> 2.09 us
    pallas_call x1, Pallas kernels: 106 us -> 102 us  [body(): pl.pallas_call(kernel, out_shape=jax.ShapeDtypeStruct((24, 64, 256), BF),...]
    unnamed x2 -> x1, local copies, waits for them, and re-layouts: 3.72 us -> 2.09 us
where the time goes in v6:
time: 104 us
  Pallas kernels  102 us (98%)
  local copies, waits for them, and re-layouts  2.09 us (2%)
    pallas_call x1, Pallas kernels, body(): pl.pallas_call(kernel, out_shape=jax.ShapeDtypeStruct((24, 64, 256), BF),...  102 us
    unnamed x1, local copies, waits for them, and re-layouts  2.09 us

profile of v6, /device:TPU:127, one launch (start us, length us, event | category | flops | bytes accessed | tf_op | source)
XLA Modules:
  0.0 103.7 jit_solution(8518476278023891503)
XLA Ops:
  0.0 101.6 %shard_map.82 = bf16[24,64,256]{2,1,0:T(8,128)(2,1)} custom-call(bf16[40,64,256]{2,1,0:T(8,128)(2,1)} %fields.1, s32[64,256]{1,0:T(8,128)} %sea.1, s32[16,128]{1,0:T(8,128)} %bitcast.5, bf16[40,192]{1,0:T(8,128)(2,1)} %embed.1, f32[49,2,24]{2,1,0:T(2,128)} %bitcast.4, bf16[2,24]{1,0:T(2,128)(2,1)} %ln_gain.1, bf16[2,96,192]{2,1,0:T(8,128)(2,1)} %up.1, ...), custom_call_target="tpu_custom_call" | custom-call | tf_op jit(solution)/shard_map/pallas_call | solution.py:646
  101.6 2.1 %copy.10 = bf16[24,64,256]{2,1,0:T(8,128)(2,1)} copy(bf16[24,64,256]{2,1,0:T(8,128)(2,1)} %shard_map.82) | data formatting | bytes 1572864

commit v7 on v6

--- a/solution.py
+++ b/solution.py
@@ -214,11 +214,6 @@
                     end_taps[b, a * 3 + d, ch, :] = jnp.where(west16, wide[a * 7 + d], wide[a * 7 + 4 + d])
 
     emb_t[...] = pe[:, :, 1].reshape(384, 192).astype(F32).T.astype(BF)
-    for k in (1, 2, 3):
-        xk = lax.rem(x + k, 4)
-        arrived(w_own.at[xk], r_w.at[10 + xk])
-    send(w_own, w_other, s_w.at[11], r_w.at[14], device(x, y, h, t, 1 - c))
-
     own[5].wait()
     for k, flip in [(0, 0)] + others[4:] + others[:4]:
         src = ys[k] * 2 + lax.rem(h + flip, 2)
@@ -508,6 +503,11 @@
         @pl.when(n == 0)
         def _():
             rim_start(0)
+
+    for k in (1, 2, 3):
+        xk = lax.rem(x + k, 4)
+        arrived(w_own.at[xk], r_w.at[10 + xk])
+    send(w_own, w_other, s_w.at[11], r_w.at[14], device(x, y, h, t, 1 - c))
 
     @pl.loop(0, 2)
     def _(b):

time: 104 us -> 103 us (level)
  no operation moved by 1% of the time
where the time goes in v7:
time: 103 us
  Pallas kernels  101 us (98%)
  local copies, waits for them, and re-layouts  2.09 us (2%)
    pallas_call x1, Pallas kernels, body(): pl.pallas_call(kernel, out_shape=jax.ShapeDtypeStruct((24, 64, 256), BF),...  101 us
    unnamed x1, local copies, waits for them, and re-layouts  2.09 us

profile of v7, /device:TPU:127, one launch (start us, length us, event | category | flops | bytes accessed | tf_op | source)
XLA Modules:
  0.0 103.1 jit_solution(16175383881131867116)
XLA Ops:
  0.0 101.0 %shard_map.82 = bf16[24,64,256]{2,1,0:T(8,128)(2,1)} custom-call(bf16[40,64,256]{2,1,0:T(8,128)(2,1)} %fields.1, s32[64,256]{1,0:T(8,128)} %sea.1, s32[16,128]{1,0:T(8,128)} %bitcast.5, bf16[40,192]{1,0:T(8,128)(2,1)} %embed.1, f32[49,2,24]{2,1,0:T(2,128)} %bitcast.4, bf16[2,24]{1,0:T(2,128)(2,1)} %ln_gain.1, bf16[2,96,192]{2,1,0:T(8,128)(2,1)} %up.1, ...), custom_call_target="tpu_custom_call" | custom-call | tf_op jit(solution)/shard_map/pallas_call | solution.py:646
  101.0 2.1 %copy.10 = bf16[24,64,256]{2,1,0:T(8,128)(2,1)} copy(bf16[24,64,256]{2,1,0:T(8,128)(2,1)} %shard_map.82) | data formatting | bytes 1572864
